TPU v7x, 512 devices: a whole 4x8x8 slice. The times are simulated.
512 devices in a mesh: grp: 8 (over x, z_lo), fsdp: 8 (over y), seq: 8 (over z_hi, core).
Axes of the slice: x: 4, y: 8, z: 8 (z_hi: 4, z_lo: 2; z = z_hi * 2 + z_lo), core: 2. Of those that a mesh axis runs over, the one named last changes fastest.
Arguments:
- img_qkv: bfloat16 [64, 1024, 3, 2048], P(('grp', 'fsdp'), 'seq'), may hold values from -15 to 15
- txt_kv: bfloat16 [64, 256, 2, 2048], P(None, ('grp', 'fsdp'), None, 'seq'), may hold values from -15 to 15
- cot_img: bfloat16 [64, 1024, 2048], P(('grp', 'fsdp'), 'seq'), may hold values from -6 to 6
- timesteps: int32 [64], P(('grp', 'fsdp')), may hold values from 0 to 999
- lengths: int32 [64], P(('grp', 'fsdp')), may hold values from 1 to 256
- gate_w: bfloat16 [256, 2048], P(None, 'seq'), may hold values from -0.375 to 0.375
- gain_q: float32 [128], replicated, may hold values from 0.1 to 1.9
- gain_k: float32 [128], replicated, may hold values from 0.1 to 1.9
- gain_t: float32 [128], replicated, may hold values from 0.1 to 1.9
Outputs:
- out_img: bfloat16 [64, 1024, 2048], P(('grp', 'fsdp'), 'seq')
- d_img_qkv: bfloat16 [64, 1024, 3, 2048], P(('grp', 'fsdp'), 'seq')
- d_txt_kv: bfloat16 [64, 256, 2, 2048], P(None, ('grp', 'fsdp'), None, 'seq')
All inputs are finite; a program needn't handle non-finite values.
Results may differ from a plain program's by a relative error of at most 0.0085.
Values may be sent and summed in bfloat16 or wider, within the bound.
No kernel may reach another device: no remote copies, remote signals or barrier semaphores. Data moves between devices by JAX's collectives and lax.ppermute only.
A program may use at most 64 MiB of HBM per device.

v0:
```python
import math

import jax
import jax.numpy as jnp
from jax import lax
from jax.sharding import PartitionSpec as P

D = 2048
HEADS = 16


norm_eps = 1e-06


def normed(vector, scale_gain):
    vector_wide = vector.astype(jnp.float32)
    inverse_rms = lax.rsqrt(jnp.mean(vector_wide * vector_wide, axis=-1, keepdims=True) + norm_eps)
    return (vector_wide * inverse_rms * scale_gain).astype(jnp.bfloat16)


def norm_back(vector, scale_gain, upstream_grad):
    vector_wide = vector.astype(jnp.float32)
    inverse_rms = lax.rsqrt(jnp.mean(vector_wide * vector_wide, axis=-1, keepdims=True) + norm_eps)
    weighted = upstream_grad * scale_gain
    cubed = inverse_rms * inverse_rms * inverse_rms
    along = jnp.mean(vector_wide * weighted, axis=-1, keepdims=True)
    return (weighted * inverse_rms - vector_wide * cubed * along).astype(jnp.bfloat16)


def embedding(stamps, half_freq):
    frequency = jnp.exp(-math.log(10000.0) * jnp.arange(half_freq, dtype=jnp.float32) / half_freq)
    angles = stamps.astype(jnp.float32)[..., None] * frequency
    return jnp.concatenate([jnp.cos(angles), jnp.sin(angles)], axis=-1)


def attend(
    queries,
    keys_img,
    values_img,
    keys_txt,
    values_txt,
    cotangent,
    gate_heads,
    prompt_len,
    gain_q,
    gain_k,
    gain_t,
):
    query_rows, head_count, head_size = queries.shape
    score_scale = 1.0 / math.sqrt(head_size)
    query_norm = normed(queries, gain_q)
    key_norm = normed(keys_img, gain_k)
    text_norm = normed(keys_txt, gain_t)
    exp_image = jnp.exp(
        jnp.einsum("qhd,khd->hqk", query_norm, key_norm, preferred_element_type=jnp.float32)
        * score_scale
    )
    positions = jnp.arange(keys_txt.shape[0], dtype=jnp.int32)
    raw_text = jnp.exp(
        jnp.einsum("qhd,khd->hqk", query_norm, text_norm, preferred_element_type=jnp.float32)
        * score_scale
    )
    exp_text = jnp.where((positions < prompt_len)[None, None, :], raw_text, 0.0)
    denom_sum = jnp.sum(exp_image, axis=-1) + jnp.sum(exp_text, axis=-1)
    prob_image = exp_image / denom_sum[:, :, None]
    weight_image = prob_image.astype(jnp.bfloat16)
    prob_text = exp_text / denom_sum[:, :, None]
    weight_text = prob_text.astype(jnp.bfloat16)
    attention = jnp.einsum(
        "hqk,khd->qhd", weight_image, values_img, preferred_element_type=jnp.float32
    ) + jnp.einsum("hqk,khd->qhd", weight_text, values_txt, preferred_element_type=jnp.float32)
    gated_out = (attention * gate_heads).astype(jnp.bfloat16)
    grad_attention = (cotangent.astype(jnp.float32) * gate_heads).astype(jnp.bfloat16)
    row_delta = jnp.sum(grad_attention.astype(jnp.float32) * attention, axis=-1).T
    grad_value = jnp.einsum(
        "hqk,qhd->khd", weight_image, grad_attention, preferred_element_type=jnp.float32
    ).astype(jnp.bfloat16)
    grad_prob = jnp.einsum(
        "qhd,khd->hqk", grad_attention, values_img, preferred_element_type=jnp.float32
    )
    grad_score = (prob_image * (grad_prob - row_delta[:, :, None])).astype(jnp.bfloat16)
    grad_qnorm = jnp.einsum(
        "hqk,khd->qhd", grad_score, key_norm, preferred_element_type=jnp.float32
    )
    grad_knorm = (
        jnp.einsum("hqk,qhd->khd", grad_score, query_norm, preferred_element_type=jnp.float32)
        * score_scale
    )
    grad_tvalue = jnp.einsum(
        "hqk,qhd->khd", weight_text, grad_attention, preferred_element_type=jnp.float32
    ).astype(jnp.bfloat16)
    grad_ptext = jnp.einsum(
        "qhd,khd->hqk", grad_attention, values_txt, preferred_element_type=jnp.float32
    )
    grad_stext = (prob_text * (grad_ptext - row_delta[:, :, None])).astype(jnp.bfloat16)
    running = jnp.einsum("hqk,khd->qhd", grad_stext, text_norm, preferred_element_type=jnp.float32)
    grad_tkey = norm_back(
        keys_txt,
        gain_t,
        jnp.einsum("hqk,qhd->khd", grad_stext, query_norm, preferred_element_type=jnp.float32)
        * score_scale,
    )
    grad_query = norm_back(queries, gain_q, (grad_qnorm + running) * score_scale)
    grad_key = norm_back(keys_img, gain_k, grad_knorm)
    return (gated_out, grad_query, grad_key, grad_value, grad_tkey, grad_tvalue)


def local(img_qkv, txt_kv, cot_img, timesteps, lengths, gate_w, gain_q, gain_k, gain_t):
    head_size = D // HEADS
    width_here = gate_w.shape[1]
    heads_here = width_here // head_size
    seq_count = lax.axis_size("seq")
    samples = txt_kv.shape[0]
    text_rows = txt_kv.shape[1]
    own_rows = img_qkv.shape[1]
    prompt_in = lax.all_to_all(
        txt_kv[:, None], ("grp", "fsdp"), split_axis=0, concat_axis=1, tiled=True
    )
    prompt = prompt_in.reshape(-1, 2, heads_here, head_size)
    prompt_rows = prompt.shape[0]
    embedded = embedding(timesteps, gate_w.shape[0] // 2)
    gate_heads = jnp.dot(
        embedded, gate_w.astype(jnp.float32), precision=lax.Precision.HIGHEST
    ).reshape(heads_here, head_size)
    heads_in, cotan_heads = (
        lax.all_to_all(img_qkv, "seq", split_axis=3, concat_axis=1, tiled=True),
        lax.all_to_all(cot_img[:, :, None, :], "seq", split_axis=3, concat_axis=1, tiled=True),
    )
    query_rows = heads_in.shape[1]
    image_part = heads_in[0].reshape(query_rows, 3, heads_here, head_size)
    cotangent = cotan_heads[0, :, 0].reshape(query_rows, heads_here, head_size)
    results = attend(
        image_part[:, 0],
        image_part[:, 1],
        image_part[:, 2],
        prompt[:, 0],
        prompt[:, 1],
        cotangent,
        gate_heads,
        lengths[0],
        gain_q,
        gain_k,
        gain_t,
    )
    gated_out, grad_query, grad_key, grad_value, grad_tkey, grad_tvalue = results
    back_image = jnp.stack([grad_query, grad_key, grad_value], axis=1).reshape(
        1, query_rows, 3, width_here
    )
    tokens_out, grad_image = (
        lax.all_to_all(
            gated_out.reshape(1, query_rows, 1, width_here),
            "seq",
            split_axis=1,
            concat_axis=3,
            tiled=True,
        ),
        lax.all_to_all(back_image, "seq", split_axis=1, concat_axis=3, tiled=True),
    )
    out_img = tokens_out.reshape(1, own_rows, width_here * seq_count)
    grad_prompt = jnp.stack([grad_tkey, grad_tvalue], axis=1).reshape(prompt_rows, 2, width_here)
    returned_txt = lax.all_to_all(
        grad_prompt.reshape(1, samples, text_rows, 2, width_here),
        ("grp", "fsdp"),
        split_axis=1,
        concat_axis=0,
        tiled=True,
    )
    return (out_img, grad_image, returned_txt.reshape(samples, text_rows, 2, width_here))


def solution(mesh):
    in_specs = (
        P(("grp", "fsdp"), "seq", None, None),
        P(None, ("grp", "fsdp"), None, "seq"),
        P(("grp", "fsdp"), "seq", None),
        P(("grp", "fsdp")),
        P(("grp", "fsdp")),
        P(None, "seq"),
        P(),
        P(),
        P(),
    )
    out_specs = (
        P(("grp", "fsdp"), "seq", None),
        P(("grp", "fsdp"), "seq", None, None),
        P(None, ("grp", "fsdp"), None, "seq"),
    )
    return jax.shard_map(local, mesh=mesh, in_specs=in_specs, out_specs=out_specs, check_vma=False)
```

profile of v0, /device:TPU:6, one launch (start us, length us, event | category | flops | bytes accessed | tf_op | source)
XLA Modules:
  0.0 246.3 jit_solution(6847165220883994497)
XLA Ops:
  0.6 12.8 %all-to-all-start.1 = ((bf16[64,1,4,2,256]{4,3,2,1,0:T(2,128)(2,1)}), bf16[64,1,4,2,256]{4,3,2,1,0:T(2,128)(2,1)S(1)}, u32[]{:S(2)}, u32[]{:S(2)}) async-start(bf16[64,1,4,2,256]{4,3,2,1,0:T(2,128)(2,1)} %bitcast.154), calls=%async_computation.1 | async-start | bytes 524288 | tf_op jit(solution)/shard_map/all_to_all | solution.py:116
  13.4 2.4 copy.143
  16.3 11.5 %reduce = bf16[2048,128]{1,0:T(8,128)(2,1)S(1)} reduce(bf16[2048,1,1,128]{3,2,1,0:T(2,128)(2,1)S(1)} %bitcast.143, bf16[]{:T(256)} %broadcast.154), dimensions={1,2}, to_apply=%bitcast.106.reduce_sub_computation | reduce | bytes 1048578
  27.8 0.9 reshape.170
  28.7 9.4 %all-to-all-start.3 = ((bf16[8,2,16384]{2,1,0:T(2,128)(2,1)}), bf16[8,2,16384]{2,1,0:T(2,128)(2,1)S(1)}, u32[]{:S(2)}, u32[]{:S(2)}) async-start(bf16[8,2,16384]{2,1,0:T(2,128)(2,1)} %reshape.170), calls=%async_computation.3 | async-start | bytes 1048576 | tf_op jit(solution)/shard_map/all_to_all | solution.py:127
  38.1 2.5 %copy.131 = bf16[1,128,3,2048]{1,2,0,3:T(4,128)(2,1)} copy(bf16[1,128,3,2048]{3,1,2,0:T(8,128)(2,1)S(1)} %copy-done.4) | data formatting | bytes 3145728 | tf_op args[0]
  40.7 15.8 %all-to-all-done.3 = bf16[8,2,16384]{2,1,0:T(2,128)(2,1)S(1)} async-done(((bf16[8,2,16384]{2,1,0:T(2,128)(2,1)}), bf16[8,2,16384]{2,1,0:T(2,128)(2,1)S(1)}, u32[]{:S(2)}, u32[]{:S(2)}) %all-to-all-start.3) | async-done | bytes 524320 | tf_op jit(solution)/shard_map/all_to_all | solution.py:127
  56.5 0.8 copy-done.3
  57.3 3.8 %all-to-all-start = ((bf16[1,128,3,2048]{1,2,0,3:T(4,128)(2,1)}), bf16[1,128,3,2048]{1,2,0,3:T(4,128)(2,1)S(1)}, u32[]{:S(2)}, u32[]{:S(2)}) async-start(bf16[1,128,3,2048]{1,2,0,3:T(4,128)(2,1)} %copy.131), calls=%async_computation | async-start | bytes 4194304 | tf_op jit(solution)/shard_map/all_to_all | solution.py:126
  64.8 0.7 fusion.35
  66.8 2.2 reshape.171
  69.0 1.1 bitcast_convert_fusion
  70.8 1.1 reshape.164
  71.9 40.1 %all-to-all-done = bf16[1,128,3,2048]{1,2,0,3:T(4,128)(2,1)S(1)} async-done(((bf16[1,128,3,2048]{1,2,0,3:T(4,128)(2,1)}), bf16[1,128,3,2048]{1,2,0,3:T(4,128)(2,1)S(1)}, u32[]{:S(2)}, u32[]{:S(2)}) %all-to-all-start) | async-done | bytes 1572896 | tf_op jit(solution)/shard_map/all_to_all | solution.py:126
  112.0 2.4 copy.196
  114.5 2.6 %reshape_squeeze.4 = bf16[1024,3,2,128]{0,3,2,1:T(8,128)(2,1)S(1)} reshape(bf16[1,8,128,3,256]{2,1,4,3,0:T(8,128)(2,1)} %bitcast.141) | data formatting | bytes 3145728 | tf_op jit(solution)/shard_map/reshape;squeeze | solution.py:130
  118.0 1.5 fusion.1
  120.2 1.4 fusion.2
  122.4 1.2 copy-done.1
  123.7 1.5 multiply_reduce_fusion
  125.2 2.5 %multiply_convert_fusion = bf16[2,1024,1024]{1,2,0:T(8,128)(2,1)S(1)} fusion(f32[2,1024]{1,0:T(2,128)S(1)} %bitcast.156, bf16[1024,2,128]{0,2,1:T(8,128)(2,1)S(1)} %get-tuple-element.20, f32[2,1024]{1,0:T(2,128)S(1)} %add.56, f32[2,1024,1024]{1,2,0:T(8,128)S(1)} %get-tuple-element.33, bf16[1024,3,2,128]{0,3,2,1:T(8,128)(2,1)S(1)} %reshape_squeeze.4), kind=kOutput, calls=%fused_computation | convolution fusion | flops 547356672 | bytes 13647872 | tf_op jit(solution)/shard_map/qhd,khd->hqk/dot_general | solution.py:78
  127.7 1.8 multiply_convert_fusion.1
  130.1 1.8 fusion.40
  131.9 1.5 fusion.6
  133.7 1.7 fusion.34
  135.9 0.8 copy.163
  136.7 11.3 %all-to-all-start.5 = ((bf16[1,64,4,2,256]{4,2,3,0,1:T(4,128)(2,1)}), bf16[1,64,4,2,256]{4,2,3,0,1:T(4,128)(2,1)}, u32[]{:S(2)}, u32[]{:S(2)}) async-start(bf16[1,64,4,2,256]{4,2,3,0,1:T(4,128)(2,1)} %copy.163), calls=%async_computation.5 | async-start | bytes 524288 | tf_op jit(solution)/shard_map/all_to_all | solution.py:161
  148.0 3.1 %fusion.17 = (f32[1024,2]{0,1:T(2,128)S(1)}, f32[1024,2]{0,1:T(2,128)S(1)}, f32[1024,2,128]{0,2,1:T(8,128)}) fusion(bf16[1024,3,2,128]{0,3,2,1:T(8,128)(2,1)S(1)} %reshape_squeeze.4, f32[1024,2,128]{0,2,1:T(8,128)S(1)} %fusion.6, f32[128]{0:T(128)S(1)} %copy-done.25, f32[2,128,1024]{2,1,0:T(8,128)} %fusion.40, ...), kind=kOutput, calls=%fused_computation.37 | convolution fusion | flops 136572928 | bytes 5393408 | tf_op jit(solution)/shard_map/hqk,khd->qhd/dot_general | solution.py:96
  151.1 2.0 copy.141
  153.1 4.7 %reduce.1 = bf16[1024,256]{1,0:T(8,128)(2,1)S(1)} reduce(bf16[1024,1,1,256]{3,2,1,0:T(2,128)(2,1)} %bitcast.144, bf16[]{:T(256)} %broadcast.154), dimensions={1,2}, to_apply=%bitcast.104.reduce_sub_computation | reduce | bytes 1048578
  157.8 0.9 reshape.168
  158.7 3.9 %convolution_convert_fusion = bf16[2,128,1024]{2,1,0:T(8,128)(2,1)S(1)} fusion(bf16[1024,2,128]{0,2,1:T(8,128)(2,1)} %copy-done.6, bf16[2,1024,1024]{1,2,0:T(8,128)(2,1)} %copy-done.1), kind=kOutput, calls=%fused_computation.26 | convolution fusion | flops 537133056 | bytes 5242880 | tf_op jit(solution)/shard_map/hqk,qhd->khd/dot_general | solution.py:75
  162.7 4.4 %all-to-all-start.2 = ((bf16[8,2,16384]{2,1,0:T(2,128)(2,1)}), bf16[8,2,16384]{2,1,0:T(2,128)(2,1)}, u32[]{:S(2)}, u32[]{:S(2)}) async-start(bf16[8,2,16384]{2,1,0:T(2,128)(2,1)} %reshape.168), calls=%async_computation.2 | async-start | bytes 1048576 | tf_op jit(solution)/shard_map/all_to_all | solution.py:150
  167.1 2.0 copy.157
  169.1 2.5 fusion.16
  171.6 0.8 copy.156
  172.4 2.4 copy.155
  174.8 4.6 %pad_maximum_fusion = bf16[1,1024,3,256]{3,2,0,1:T(4,128)(2,1)} fusion(bf16[1,1024,1,256]{3,2,0,1:T(2,128)(2,1)S(1)} %copy-done.2, bf16[1,1024,1,256]{3,2,0,1:T(2,128)(2,1)S(1)} %copy.156, bf16[1,1024,1,256]{3,2,0,1:T(2,128)(2,1)S(1)} %copy.155), kind=kLoop, calls=%fused_computation.5 | loop fusion | flops 4718592 | bytes 3145728 | tf_op jit(solution)/shard_map/stack | solution.py:146
  179.4 5.8 %all-to-all-done.2 = bf16[8,2,16384]{2,1,0:T(2,128)(2,1)} async-done(((bf16[8,2,16384]{2,1,0:T(2,128)(2,1)}), bf16[8,2,16384]{2,1,0:T(2,128)(2,1)}, u32[]{:S(2)}, u32[]{:S(2)}) %all-to-all-start.2) | async-done | bytes 524320 | tf_op jit(solution)/shard_map/all_to_all | solution.py:150
  185.2 3.6 %all-to-all-start.4 = ((bf16[1,1024,3,256]{3,2,0,1:T(4,128)(2,1)}), bf16[1,1024,3,256]{3,2,0,1:T(4,128)(2,1)S(1)}, u32[]{:S(2)}, u32[]{:S(2)}) async-start(bf16[1,1024,3,256]{3,2,0,1:T(4,128)(2,1)} %pad_maximum_fusion), calls=%async_computation.4 | async-start | bytes 4194304 | tf_op jit(solution)/shard_map/all_to_all | solution.py:157
  188.8 1.9 copy.165
  190.7 2.2 reshape.169
  192.9 0.9 copy.186
  193.8 1.3 copy.142
  195.1 1.0 copy.164
  196.1 44.1 %all-to-all-done.4 = bf16[1,1024,3,256]{3,2,0,1:T(4,128)(2,1)S(1)} async-done(((bf16[1,1024,3,256]{3,2,0,1:T(4,128)(2,1)}), bf16[1,1024,3,256]{3,2,0,1:T(4,128)(2,1)S(1)}, u32[]{:S(2)}, u32[]{:S(2)}) %all-to-all-start.4) | async-done | bytes 1572896 | tf_op jit(solution)/shard_map/all_to_all | solution.py:157
  240.2 2.3 copy.158
  242.5 3.7 %all_to_all.67 = bf16[1,128,3,2048]{3,1,2,0:T(8,128)(2,1)} reshape(bf16[1,128,3,8,256]{4,3,1,2,0:T(8,128)(2,1)} %copy.158) | data formatting | bytes 3145728 | tf_op jit(solution)/shard_map/all_to_all | solution.py:157
  (84 shorter events, 8.5 us)
Async XLA Ops:
  0.6 64.2 %copy-start = (bf16[256,256]{1,0:T(8,128)(2,1)S(1)}, bf16[256,256]{1,0:T(8,128)(2,1)}, u32[]{:S(2)}) copy-start(bf16[256,256]{1,0:T(8,128)(2,1)} %param.14) | copy-start | bytes 393220
  0.6 28.1 %all-to-all-start.1 = ((bf16[64,1,4,2,256]{4,3,2,1,0:T(2,128)(2,1)}), bf16[64,1,4,2,256]{4,3,2,1,0:T(2,128)(2,1)S(1)}, u32[]{:S(2)}, u32[]{:S(2)}) async-start(bf16[64,1,4,2,256]{4,3,2,1,0:T(2,128)(2,1)} %bitcast.154), calls=%async_computation.1 | async-start | bytes 524288 | tf_op jit(solution)/shard_map/all_to_all | solution.py:116
  15.8 22.4 %copy-start.4 = (bf16[1,128,3,2048]{3,1,2,0:T(8,128)(2,1)S(1)}, bf16[1,128,3,2048]{3,1,2,0:T(8,128)(2,1)}, u32[]{:S(2)}) copy-start(bf16[1,128,3,2048]{3,1,2,0:T(8,128)(2,1)} %param.9) | copy-start | bytes 4718596
  28.7 27.8 %all-to-all-start.3 = ((bf16[8,2,16384]{2,1,0:T(2,128)(2,1)}), bf16[8,2,16384]{2,1,0:T(2,128)(2,1)S(1)}, u32[]{:S(2)}, u32[]{:S(2)}) async-start(bf16[8,2,16384]{2,1,0:T(2,128)(2,1)} %reshape.170), calls=%async_computation.3 | async-start | bytes 1048576 | tf_op jit(solution)/shard_map/all_to_all | solution.py:127
  40.7 22.3 %copy-start.13 = (f32[128]{0:T(128)S(1)}, f32[128]{0:T(128)}, u32[]{:S(2)}) copy-start(f32[128]{0:T(128)} %param.16) | copy-start | bytes 1540
  40.7 22.9 %copy-start.17 = (f32[128]{0:T(128)S(1)}, f32[128]{0:T(128)}, u32[]{:S(2)}) copy-start(f32[128]{0:T(128)} %param.15) | copy-start | bytes 1540
  40.7 23.5 %copy-start.22 = (f32[128]{0:T(128)S(1)}, f32[128]{0:T(128)}, u32[]{:S(2)}) copy-start(f32[128]{0:T(128)} %param.17) | copy-start | bytes 1540
  56.5 0.8 copy-start.3
  57.3 54.7 %all-to-all-start = ((bf16[1,128,3,2048]{1,2,0,3:T(4,128)(2,1)}), bf16[1,128,3,2048]{1,2,0,3:T(4,128)(2,1)S(1)}, u32[]{:S(2)}, u32[]{:S(2)}) async-start(bf16[1,128,3,2048]{1,2,0,3:T(4,128)(2,1)} %copy.131), calls=%async_computation | async-start | bytes 4194304 | tf_op jit(solution)/shard_map/all_to_all | solution.py:126
  114.5 3.5 %copy-start.14 = (f32[128]{0:T(128)S(1)}, f32[128]{0:T(128)}, u32[]{:S(2)}) copy-start(f32[128]{0:T(128)} %param.16) | copy-start | bytes 1540
  114.5 3.5 %copy-start.18 = (f32[128]{0:T(128)S(1)}, f32[128]{0:T(128)}, u32[]{:S(2)}) copy-start(f32[128]{0:T(128)} %param.15) | copy-start | bytes 1540
  117.9 1.5 copy-start.10
  118.0 1.5 copy-start.23
  118.0 1.5 copy-start.27
  121.6 2.0 copy-start.1
  121.7 2.0 copy-start.5
  121.7 2.0 copy-start.21
  125.2 4.3 %copy-start.6 = (bf16[1024,2,128]{0,2,1:T(8,128)(2,1)}, bf16[1024,2,128]{0,2,1:T(8,128)(2,1)S(1)}, u32[]{:S(2)}) copy-start(bf16[1024,2,128]{0,2,1:T(8,128)(2,1)S(1)} %get-tuple-element.20) | copy-start | bytes 1572868
  129.4 0.7 copy-start.15
  130.1 1.8 copy-start.19
  130.1 1.8 copy-start.20
  131.9 1.8 copy-start.26
  133.4 2.0 copy-start.11
  133.4 2.0 copy-start.16
  133.6 14.4 %copy-start.12 = (f32[256,2]{0,1:T(2,128)S(1)}, f32[256,2]{0,1:T(2,128)}, u32[]{:S(2)}) copy-start(f32[256,2]{0,1:T(2,128)} %get-tuple-element.31) | copy-start | bytes 6148
  133.7 14.4 %copy-start.24 = (f32[128]{0:T(128)S(1)}, f32[128]{0:T(128)}, u32[]{:S(2)}) copy-start(f32[128]{0:T(128)} %param.17) | copy-start | bytes 1540
  133.7 14.4 %copy-start.25 = (f32[128]{0:T(128)S(1)}, f32[128]{0:T(128)}, u32[]{:S(2)}) copy-start(f32[128]{0:T(128)} %broadcast_multiply_fusion.5) | copy-start | bytes 1540
  136.7 25.9 %all-to-all-start.5 = ((bf16[1,64,4,2,256]{4,2,3,0,1:T(4,128)(2,1)}), bf16[1,64,4,2,256]{4,2,3,0,1:T(4,128)(2,1)}, u32[]{:S(2)}, u32[]{:S(2)}) async-start(bf16[1,64,4,2,256]{4,2,3,0,1:T(4,128)(2,1)} %copy.163), calls=%async_computation.5 | async-start | bytes 524288 | tf_op jit(solution)/shard_map/all_to_all | solution.py:161
  148.0 3.1 %copy-start.7 = (bf16[1024,2,128]{0,2,1:T(8,128)(2,1)S(1)}, bf16[1024,2,128]{0,2,1:T(8,128)(2,1)}, u32[]{:S(2)}) copy-start(bf16[1024,2,128]{0,2,1:T(8,128)(2,1)} %get-tuple-element.23) | copy-start | bytes 1572868
  162.6 6.5 %copy-start.8 = (f32[1024,2]{0,1:T(2,128)S(1)}, f32[1024,2]{0,1:T(2,128)}, u32[]{:S(2)}) copy-start(f32[1024,2]{0,1:T(2,128)} %get-tuple-element.28) | copy-start | bytes 24580
  162.6 6.5 %copy-start.9 = (f32[1024,2]{0,1:T(2,128)S(1)}, f32[1024,2]{0,1:T(2,128)}, u32[]{:S(2)}) copy-start(f32[1024,2]{0,1:T(2,128)} %get-tuple-element.42) | copy-start | bytes 24580
  162.7 22.6 %all-to-all-start.2 = ((bf16[8,2,16384]{2,1,0:T(2,128)(2,1)}), bf16[8,2,16384]{2,1,0:T(2,128)(2,1)}, u32[]{:S(2)}, u32[]{:S(2)}) async-start(bf16[8,2,16384]{2,1,0:T(2,128)(2,1)} %reshape.168), calls=%async_computation.2 | async-start | bytes 1048576 | tf_op jit(solution)/shard_map/all_to_all | solution.py:150
  171.6 3.3 %copy-start.2 = (bf16[1,1024,1,256]{3,2,0,1:T(2,128)(2,1)S(1)}, bf16[1,1024,1,256]{3,2,0,1:T(2,128)(2,1)}, u32[]{:S(2)}) copy-start(bf16[1,1024,1,256]{3,2,0,1:T(2,128)(2,1)} %copy.157) | copy-start | bytes 1572868
  185.2 55.0 %all-to-all-start.4 = ((bf16[1,1024,3,256]{3,2,0,1:T(4,128)(2,1)}), bf16[1,1024,3,256]{3,2,0,1:T(4,128)(2,1)S(1)}, u32[]{:S(2)}, u32[]{:S(2)}) async-start(bf16[1,1024,3,256]{3,2,0,1:T(4,128)(2,1)} %pad_maximum_fusion), calls=%async_computation.4 | async-start | bytes 4194304 | tf_op jit(solution)/shard_map/all_to_all | solution.py:157
where the time goes:
time: 247 us; the launch traced here: 246 us
  waiting for transfers between devices  106 us (43%)
  starting transfers between devices  45.2 us (18%)
  local copies, waits for them, and re-layouts  40.7 us (16%)
  other arithmetic  30 us (12%)
  matrix products  22 us (9%)
    all_to_all x1, waiting for transfers between devices, local(): lax.all_to_all(back_image, 'seq', split_axis=1, concat_axis=3, tiled=True)  44.1 us
    all_to_all x1, waiting for transfers between devices, local(): lax.all_to_all(img_qkv, 'seq', split_axis=3, concat_axis=1, tiled=True)  40.1 us
    unnamed x2, other arithmetic  16.3 us
    all_to_all x1, waiting for transfers between devices, local(): lax.all_to_all(cot_img[:, :, None, :], 'seq', split_axis=3, concat_axis=1...  15.8 us
    unnamed x67, local copies, waits for them, and re-layouts  15.5 us
    all_to_all x1, starting transfers between devices, local(): lax.all_to_all(txt_kv[:, None], ('grp', 'fsdp'), split_axis=0, concat_axi...  12.8 us
    all_to_all x1, starting transfers between devices, local(): lax.all_to_all(grad_prompt.reshape(1, samples, text_rows, 2, width_here),...  11.3 us
    all_to_all x1, starting transfers between devices, local(): lax.all_to_all(cot_img[:, :, None, :], 'seq', split_axis=3, concat_axis=1...  9.41 us
  transfers between devices with their start and end apart: 6, of which 4 were waited for; matrix products, arithmetic and copies ran while one was open for 25% of the time, Pallas kernels for 0%

commit v1 on v0

v1 whole, which is shorter than its diff:
```python
import math

import jax
import jax.numpy as jnp
from jax import lax
from jax.experimental import pallas as pl
from jax.experimental.pallas import tpu as pltpu
from jax.sharding import PartitionSpec as P

D = 2048
HEADS = 16
HS = D // HEADS
EPS = 1e-06
SCALE = 1.0 / math.sqrt(HS)
EXP2_SCALE = SCALE * math.log2(math.e)
CHIPS = 4
SEQ = 2 * CHIPS
OFFSETS = ((2, 0), (2, 1), (1, 0), (3, 0), (1, 1), (3, 1), (0, 1), (0, 0))
ROWS = 128
WIDTH = 256
HPD = WIDTH // HS
L = SEQ * ROWS
PROMPT = 256
KEYS = L + PROMPT
BLOCK = 2
QROWS = BLOCK * ROWS


def embedding(stamps, half_freq):
    frequency = jnp.exp(-math.log(10000.0) * jnp.arange(half_freq, dtype=jnp.float32) / half_freq)
    angles = stamps.astype(jnp.float32)[..., None] * frequency
    return jnp.concatenate([jnp.cos(angles), jnp.sin(angles)], axis=-1)


def normed(x, gain):
    r = lax.rsqrt(jnp.mean(x * x, axis=-1, keepdims=True) + EPS)
    return (x * r * gain).astype(jnp.bfloat16)


def norm_back(x, gain, upstream):
    r = lax.rsqrt(jnp.mean(x * x, axis=-1, keepdims=True) + EPS)
    weighted = upstream * gain
    along = jnp.mean(x * weighted, axis=-1, keepdims=True)
    return (weighted * r - x * (r * r * r * along)).astype(jnp.bfloat16)


def dot(a, b, dims):
    return lax.dot_general(a, b, (dims, ((), ())), preferred_element_type=jnp.float32)


NT = ((1,), (1,))
NN = ((1,), (0,))


def position():
    me = lax.axis_index("seq")
    return me // 2, me % 2


def partner(i, c, offset):
    dz, dc = offset
    return ((i + dz) % CHIPS) * 2 + (c + dc) % 2


def pack_kernel(place, img, cot, *outs):
    for offset, out in zip(OFFSETS, outs):
        d = partner(place[0], place[1], offset)
        columns = pl.ds(pl.multiple_of(d * WIDTH, WIDTH), WIDTH)
        out[:3] = img[:, :, columns]
        out[3] = cot[:, columns]


def unpack_kernel(place, *refs):
    packed, (out, grads) = refs[:SEQ], refs[SEQ:]
    for offset, part in zip(OFFSETS, packed):
        d = partner(place[0], place[1], offset)
        columns = pl.ds(pl.multiple_of(d * WIDTH, WIDTH), WIDTH)
        out[:, columns] = part[0]
        grads[:, :, columns] = part[1:]


def attend_kernel(length, txt, gate, gain_q, gain_k, gain_t, *refs):
    received, sent, d_txt = refs[:SEQ], refs[SEQ : 2 * SEQ], refs[2 * SEQ]
    rin, rout, kn, kt, ve, vt, dk, dv, sems = refs[2 * SEQ + 1 :]
    copies = [pltpu.make_async_copy(r, rin.at[s], sems.at[s]) for s, r in enumerate(received)]
    for copy in copies:
        copy.start()
    for copy in copies:
        copy.wait()
    gq, gk, gt = gain_q[...], gain_k[...], gain_t[...]
    live = lax.broadcasted_iota(jnp.int32, (PROMPT, HS), 0) < length[0]
    lane = lax.broadcasted_iota(jnp.int32, (QROWS, HS), 1)
    for h in range(HPD):
        columns = pl.ds(h * HS, HS)
        gate_h = gate[:, columns]
        k_img = rin[:, 1, :, columns].reshape(L, HS).astype(jnp.float32)
        kn[:L] = normed(k_img, gk)
        kn[L:] = normed(txt[:, 0, columns].astype(jnp.float32), gt)
        ve[:L, :HS] = rin[:, 2, :, columns].reshape(L, HS)
        ve[:L, HS:] = jnp.ones((L, HS), jnp.bfloat16)
        ve[L:, :HS] = jnp.where(live, txt[:, 1, columns].astype(jnp.float32), 0.0).astype(jnp.bfloat16)
        ve[L:, HS:] = jnp.where(live, 1.0, 0.0).astype(jnp.bfloat16)
        kt[...] = kn[...].T
        vt[...] = ve[...].T
        dk[...] = jnp.zeros_like(dk)
        dv[...] = jnp.zeros_like(dv)

        def step(j, carry):
            rows = pl.ds(j * BLOCK, BLOCK)
            q = rin[rows, 0, :, columns].reshape(QROWS, HS).astype(jnp.float32)
            cot = rin[rows, 3, :, columns].reshape(QROWS, HS).astype(jnp.float32)
            qn = normed(q, gq)
            e = jnp.exp2(dot(kn[...], qn, NT) * EXP2_SCALE)
            eb = e.astype(jnp.bfloat16)
            sums = dot(vt[...], eb, NN).T
            rz = 1.0 / sums[:, HS:]
            attn = sums[:, :HS] * rz
            rout[rows, 0, :, columns] = (attn * gate_h).astype(jnp.bfloat16).reshape(BLOCK, ROWS, HS)
            g = (cot * gate_h * rz).astype(jnp.bfloat16)
            delta = -jnp.sum(g.astype(jnp.float32) * attn, axis=-1, keepdims=True)
            hi = delta.astype(jnp.bfloat16).astype(jnp.float32)
            mid = (delta - hi).astype(jnp.bfloat16).astype(jnp.float32)
            low = delta - hi - mid
            tail = jnp.where(lane == 0, hi, jnp.where(lane == 1, mid, jnp.where(lane == 2, low, 0.0)))
            ge = jnp.concatenate([g, tail.astype(jnp.bfloat16)], axis=1)
            ds = (e * dot(ve[...], ge, NT)).astype(jnp.bfloat16)
            dv[...] += dot(eb, g, NN)
            dk[...] += dot(ds, qn, NN)
            dq = dot(kt[...], ds, NN).T * SCALE
            rout[rows, 1, :, columns] = norm_back(q, gq, dq).reshape(BLOCK, ROWS, HS)
            return carry

        lax.fori_loop(0, SEQ // BLOCK, step, 0)
        rout[:, 2, :, columns] = norm_back(k_img, gk, dk[:L] * SCALE).reshape(SEQ, ROWS, HS)
        rout[:, 3, :, columns] = dv[:L].astype(jnp.bfloat16).reshape(SEQ, ROWS, HS)
        d_txt[:, 0, columns] = norm_back(txt[:, 0, columns].astype(jnp.float32), gt, dk[L:] * SCALE)
        d_txt[:, 1, columns] = jnp.where(live, dv[L:], 0.0).astype(jnp.bfloat16)
    copies = [pltpu.make_async_copy(rout.at[s], r, sems.at[s]) for s, r in enumerate(sent)]
    for copy in copies:
        copy.start()
    for copy in copies:
        copy.wait()


MESSAGE = jax.ShapeDtypeStruct((4, ROWS, WIDTH), jnp.bfloat16)
SMEM = pl.BlockSpec(memory_space=pltpu.SMEM)
VMEM = pl.BlockSpec(memory_space=pltpu.VMEM)
ANY = pl.BlockSpec(memory_space=pl.ANY)


def attend(length, txt, gate, gain_q, gain_k, gain_t, received):
    prompt = jax.ShapeDtypeStruct((PROMPT, 2, WIDTH), jnp.bfloat16)
    results = pl.pallas_call(
        attend_kernel,
        out_shape=[MESSAGE] * SEQ + [prompt],
        in_specs=[SMEM] + [VMEM] * 5 + [ANY] * SEQ,
        out_specs=[ANY] * SEQ + [VMEM],
        scratch_shapes=[
            pltpu.VMEM((SEQ, 4, ROWS, WIDTH), jnp.bfloat16),
            pltpu.VMEM((SEQ, 4, ROWS, WIDTH), jnp.bfloat16),
            pltpu.VMEM((KEYS, HS), jnp.bfloat16),
            pltpu.VMEM((HS, KEYS), jnp.bfloat16),
            pltpu.VMEM((KEYS, 2 * HS), jnp.bfloat16),
            pltpu.VMEM((2 * HS, KEYS), jnp.bfloat16),
            pltpu.VMEM((KEYS, HS), jnp.float32),
            pltpu.VMEM((KEYS, HS), jnp.float32),
            pltpu.SemaphoreType.DMA((SEQ,)),
        ],
        compiler_params=pltpu.CompilerParams(vmem_limit_bytes=32 * 1024 * 1024),
        name="attend",
    )(length, txt, gate, gain_q, gain_k, gain_t, *received)
    return results[:SEQ], results[SEQ]


def pack(place, img, cot):
    return pl.pallas_call(
        pack_kernel,
        out_shape=[MESSAGE] * SEQ,
        in_specs=[SMEM, VMEM, VMEM],
        out_specs=[VMEM] * SEQ,
        compiler_params=pltpu.CompilerParams(vmem_limit_bytes=16 * 1024 * 1024),
        name="pack",
    )(place, img, cot)


def unpack(place, packed):
    return pl.pallas_call(
        unpack_kernel,
        out_shape=(
            jax.ShapeDtypeStruct((ROWS, D), jnp.bfloat16),
            jax.ShapeDtypeStruct((3, ROWS, D), jnp.bfloat16),
        ),
        in_specs=[SMEM] + [VMEM] * SEQ,
        out_specs=(VMEM, VMEM),
        compiler_params=pltpu.CompilerParams(vmem_limit_bytes=16 * 1024 * 1024),
        name="unpack",
    )(place, *packed)


def exchange(parts, way):
    results = []
    for offset, part in zip(OFFSETS, parts):
        if offset != (0, 0):
            pairs = [(me, partner(me // 2, me % 2, offset)) for me in range(SEQ)]
            part = lax.ppermute(part, "seq", pairs if way == 1 else [(b, a) for a, b in pairs])
        results.append(part)
    return results


def local(img_qkv, txt_kv, cot_img, timesteps, lengths, gate_w, gain_q, gain_k, gain_t):
    samples, text_rows = txt_kv.shape[:2]
    groups = ("grp", "fsdp")
    place = jnp.stack(position())
    messages = pack(place, img_qkv[0].transpose(1, 0, 2), cot_img[0])
    txt_kv, *messages = lax.optimization_barrier((txt_kv, *messages))
    received = exchange(messages, 1)
    prompt = lax.all_to_all(txt_kv, groups, split_axis=0, concat_axis=0, tiled=True)
    prompt = prompt.reshape(samples * text_rows, 2, WIDTH)
    embedded = embedding(timesteps, gate_w.shape[0] // 2)
    gate = jnp.dot(embedded, gate_w.astype(jnp.float32), precision=lax.Precision.HIGHEST)
    sent, d_txt = attend(
        lengths, prompt, gate, gain_q[None], gain_k[None], gain_t[None], received
    )
    grad_prompt = d_txt.reshape(samples, text_rows, 2, WIDTH)
    d_txt = lax.all_to_all(grad_prompt, groups, split_axis=0, concat_axis=0, tiled=True)
    out, grads = unpack(place, exchange(sent, -1))
    return out[None], grads.transpose(1, 0, 2)[None], d_txt


def solution(mesh):
    in_specs = (
        P(("grp", "fsdp"), "seq", None, None),
        P(None, ("grp", "fsdp"), None, "seq"),
        P(("grp", "fsdp"), "seq", None),
        P(("grp", "fsdp")),
        P(("grp", "fsdp")),
        P(None, "seq"),
        P(),
        P(),
        P(),
    )
    out_specs = (
        P(("grp", "fsdp"), "seq", None),
        P(("grp", "fsdp"), "seq", None, None),
        P(None, ("grp", "fsdp"), None, "seq"),
    )
    return jax.shard_map(local, mesh=mesh, in_specs=in_specs, out_specs=out_specs, check_vma=False)
```

time: 247 us -> 146 us (0.59)
  waiting for transfers between devices: 106 us -> 32 us
  starting transfers between devices: 45.2 us -> 81.2 us
  local copies, waits for them, and re-layouts: 40.7 us -> 5.3 us
  other arithmetic: 30 us -> 0.13 us
  Pallas kernels: 0 us -> 24.4 us
  matrix products: 22 us -> 0.14 us
    all_to_all x6 -> x2, waiting for transfers between devices: 106 us -> 0.01 us  [the longest x1 0.01 us: local(): lax.all_to_all(txt_kv, groups, split_axis=0, concat_axis=0, tiled=True)]
    ppermute x0 -> x14, starting transfers between devices: none -> 57.7 us  [exchange(): lax.ppermute(part, 'seq', pairs if way == 1 else [(b, a) for a, b in pairs])]
    ppermute x0 -> x14, waiting for transfers between devices: none -> 32 us  [exchange(): lax.ppermute(part, 'seq', pairs if way == 1 else [(b, a) for a, b in pairs])]
    pallas_call x0 -> x3, Pallas kernels: none -> 24.4 us  [the longest x1 20.7 us: attend(): pl.pallas_call(attend_kernel, out_shape=[MESSAGE] * SEQ + [prompt], in_sp...]
    all_to_all x6 -> x2, starting transfers between devices: 45.2 us -> 23.5 us  [the longest x1 11.8 us: local(): lax.all_to_all(grad_prompt, groups, split_axis=0, concat_axis=0, tiled=True)]
    dot_general x12 -> x0, matrix products: 21.2 us -> none  [the longest x1 3.87 us: attend(): jnp.einsum('hqk,qhd->khd', weight_image, grad_attention, preferred_elemen...]
    unnamed x2 -> x0, other arithmetic: 16.3 us -> none
    unnamed x67 -> x19, local copies, waits for them, and re-layouts: 15.5 us -> 5.3 us
  transfers between devices with their start and end apart: 6 -> 16, of which waited for: 4 -> 4; matrix products, arithmetic and copies ran while one was open for 25% -> 0% of each run, Pallas kernels for 0% -> 1%
where the time goes in v1:
time: 146 us; the launch traced here: 145 us
  starting transfers between devices  81.2 us (56%)
  waiting for transfers between devices  32 us (22%)
  Pallas kernels  24.4 us (17%)
  local copies, waits for them, and re-layouts  5.3 us (4%)
  between operations  2.22 us (2%)
    ppermute x14, starting transfers between devices, exchange(): lax.ppermute(part, 'seq', pairs if way == 1 else [(b, a) for a, b in pairs])  57.7 us
    ppermute x14, waiting for transfers between devices, exchange(): lax.ppermute(part, 'seq', pairs if way == 1 else [(b, a) for a, b in pairs])  32 us
    pallas_call x1, Pallas kernels, attend(): pl.pallas_call(attend_kernel, out_shape=[MESSAGE] * SEQ + [prompt], in_sp...  20.7 us
    all_to_all x1, starting transfers between devices, local(): lax.all_to_all(grad_prompt, groups, split_axis=0, concat_axis=0, tiled=True)  11.8 us
    all_to_all x1, starting transfers between devices, local(): lax.all_to_all(txt_kv, groups, split_axis=0, concat_axis=0, tiled=True)  11.7 us
    unnamed x19, local copies, waits for them, and re-layouts  5.3 us
  transfers between devices with their start and end apart: 16, of which 4 were waited for; matrix products, arithmetic and copies ran while one was open for 0% of the time, Pallas kernels for 1%

profile of v1, /device:TPU:6, one launch (start us, length us, event | category | flops | bytes accessed | tf_op | source)
XLA Modules:
  0.0 145.4 jit_solution(17103161745989645224)
XLA Ops:
  0.6 0.0 copy-start
  0.6 0.0 copy-start.5
  0.7 0.0 copy-start.4
  0.7 0.1 pad_add_fusion.place
  0.8 1.4 copy-done.1
  2.2 1.0 copy-done.2
  3.2 1.6 %pack.1 = (bf16[4,128,256]{2,1,0:T(8,128)(2,1)S(1)}, bf16[4,128,256]{2,1,0:T(8,128)(2,1)S(1)}, bf16[4,128,256]{2,1,0:T(8,128)(2,1)}, bf16[4,128,256]{2,1,0:T(8,1...) custom-call(s32[2]{0:T(128)S(1)} %pad_add_fusion.place, ...), custom_call_target="tpu_custom_call" | custom-call | tf_op jit(solution)/shard_map/pack/pallas_call | solution.py:176
  4.9 10.9 %collective-permute-start = (bf16[4,128,256]{2,1,0:T(8,128)(2,1)S(1)}, bf16[4,128,256]{2,1,0:T(8,128)(2,1)S(1)}, u32[]{:S(2)}, u32[]{:S(2)}) collective-permute-start(bf16[4,128,256]{2,1,0:T(8,128)(2,1)S(1)} %get-tuple-element.40), channel_id=1, source_target_pairs={{0,4},{1,5},{2,6},{3,7},{4,0},{5,1},{6,2},{7,3},{8,12},{9,13},{10,... | collective-permute-start | bytes 786440 | tf_op jit(solution)/shard_map/ppermute | solution.py:205
  15.8 1.9 %collective-permute-start.1 = (bf16[4,128,256]{2,1,0:T(8,128)(2,1)S(1)}, bf16[4,128,256]{2,1,0:T(8,128)(2,1)S(1)}, u32[]{:S(2)}, u32[]{:S(2)}) collective-permute-start(bf16[4,128,256]{2,1,0:T(8,128)(2,1)S(1)} %get-tuple-element.41), channel_id=1, source_target_pairs={{0,5},{1,4},{2,7},{3,6},{4,1},{5,0},{6,3},{7,2},{8,13},{9,12},{10,... | collective-permute-start | bytes 786440 | tf_op jit(solution)/shard_map/ppermute | solution.py:205
  17.7 11.7 %all-to-all-start = ((bf16[64,4,2,256]{3,2,1,0:T(2,128)(2,1)}), bf16[64,4,2,256]{3,2,1,0:T(2,128)(2,1)S(1)}, u32[]{:S(2)}, u32[]{:S(2)}) async-start(bf16[64,4,2,256]{3,2,1,0:T(2,128)(2,1)} %param.10), calls=%async_computation | async-start | bytes 524288 | tf_op jit(solution)/shard_map/all_to_all | solution.py:217
  29.4 4.3 %collective-permute-start.2 = (bf16[4,128,256]{2,1,0:T(8,128)(2,1)}, bf16[4,128,256]{2,1,0:T(8,128)(2,1)S(1)}, u32[]{:S(2)}, u32[]{:S(2)}) collective-permute-start(bf16[4,128,256]{2,1,0:T(8,128)(2,1)} %get-tuple-element.42), channel_id=1, source_target_pairs={{0,2},{1,3},{2,4},{3,5},{4,6},{5,7},{6,0},{7,1},{8,10},{9,11},{10,... | collective-permute-start | bytes 786440 | tf_op jit(solution)/shard_map/ppermute | solution.py:205
  33.7 4.7 %collective-permute-start.3 = (bf16[4,128,256]{2,1,0:T(8,128)(2,1)}, bf16[4,128,256]{2,1,0:T(8,128)(2,1)S(1)}, u32[]{:S(2)}, u32[]{:S(2)}) collective-permute-start(bf16[4,128,256]{2,1,0:T(8,128)(2,1)} %get-tuple-element.43), channel_id=1, source_target_pairs={{0,6},{1,7},{2,0},{3,1},{4,2},{5,3},{6,4},{7,5},{8,14},{9,15},{10,... | collective-permute-start | bytes 786440 | tf_op jit(solution)/shard_map/ppermute | solution.py:205
  38.4 2.2 %collective-permute-start.4 = (bf16[4,128,256]{2,1,0:T(8,128)(2,1)S(1)}, bf16[4,128,256]{2,1,0:T(8,128)(2,1)S(1)}, u32[]{:S(2)}, u32[]{:S(2)}) collective-permute-start(bf16[4,128,256]{2,1,0:T(8,128)(2,1)S(1)} %get-tuple-element.44), channel_id=1, source_target_pairs={{0,3},{1,2},{2,5},{3,4},{4,7},{5,6},{6,1},{7,0},{8,11},{9,10},{10,... | collective-permute-start | bytes 786440 | tf_op jit(solution)/shard_map/ppermute | solution.py:205
  41.2 0.0 collective-permute-done.refs_0_
  41.2 5.5 %collective-permute-start.5 = (bf16[4,128,256]{2,1,0:T(8,128)(2,1)S(1)}, bf16[4,128,256]{2,1,0:T(8,128)(2,1)S(1)}, u32[]{:S(2)}, u32[]{:S(2)}) collective-permute-start(bf16[4,128,256]{2,1,0:T(8,128)(2,1)S(1)} %get-tuple-element.45), channel_id=1, source_target_pairs={{0,7},{1,6},{2,1},{3,0},{4,3},{5,2},{6,5},{7,4},{8,15},{9,14},{10,... | collective-permute-start | bytes 786440 | tf_op jit(solution)/shard_map/ppermute | solution.py:205
  46.8 0.0 collective-permute-done.1.refs_1_
  46.8 2.0 %collective-permute-start.6 = (bf16[4,128,256]{2,1,0:T(8,128)(2,1)S(1)}, bf16[4,128,256]{2,1,0:T(8,128)(2,1)S(1)}, u32[]{:S(2)}, u32[]{:S(2)}) collective-permute-start(bf16[4,128,256]{2,1,0:T(8,128)(2,1)S(1)} %get-tuple-element.46), channel_id=1, source_target_pairs={{0,1},{1,0},{2,3},{3,2},{4,5},{5,4},{6,7},{7,6},{8,9},{9,8},{10,11... | collective-permute-start | bytes 786440 | tf_op jit(solution)/shard_map/ppermute | solution.py:205
  48.8 0.1 fusion.3
  49.5 0.0 copy-done
  49.5 0.1 fusion.gate
  49.6 9.4 %collective-permute-done.2.refs_2_ = bf16[4,128,256]{2,1,0:T(8,128)(2,1)S(1)} collective-permute-done((bf16[4,128,256]{2,1,0:T(8,128)(2,1)}, bf16[4,128,256]{2,1,0:T(8,128)(2,1)S(1)}, u32[]{:S(2)}, u32[]{:S(2)}) %collective-permute-start.2) | collective-permute-done | bytes 262176 | tf_op jit(solution)/shard_map/ppermute | solution.py:205
  59.0 0.0 collective-permute-done.3.refs_3_
  59.0 5.5 %collective-permute-done.4.refs_4_ = bf16[4,128,256]{2,1,0:T(8,128)(2,1)S(1)} collective-permute-done((bf16[4,128,256]{2,1,0:T(8,128)(2,1)S(1)}, bf16[4,128,256]{2,1,0:T(8,128)(2,1)S(1)}, u32[]{:S(2)}, u32[]{:S(2)}) %collective-permute-start.4) | collective-permute-done | bytes 262176 | tf_op jit(solution)/shard_map/ppermute | solution.py:205
  64.4 0.0 collective-permute-done.5.refs_5_
  64.4 0.0 collective-permute-done.6.refs_6_
  64.5 0.0 all-to-all-done
  64.5 20.7 %attend.1 = (bf16[4,128,256]{2,1,0:T(8,128)(2,1)}, bf16[4,128,256]{2,1,0:T(8,128)(2,1)}, bf16[4,128,256]{2,1,0:T(8,128)(2,1)S(1)}, bf16[4,128,256]{2,1,0:T(8,128...) custom-call(s32[1]{0:T(128)S(6)} %copy.14.length, ...), custom_call_target="tpu_custom_call" | custom-call | tf_op jit(solution)/shard_map/attend/pallas_call | solution.py:153
  85.2 0.7 copy-done.6
  85.9 0.7 copy-done.7
  86.6 0.7 copy-done.8
  87.3 7.3 %collective-permute-start.7 = (bf16[4,128,256]{2,1,0:T(8,128)(2,1)}, bf16[4,128,256]{2,1,0:T(8,128)(2,1)S(1)}, u32[]{:S(2)}, u32[]{:S(2)}) collective-permute-start(bf16[4,128,256]{2,1,0:T(8,128)(2,1)} %get-tuple-element.48), channel_id=1, source_target_pairs={{4,0},{5,1},{6,2},{7,3},{0,4},{1,5},{2,6},{3,7},{12,8},{13,9},{14,... | collective-permute-start | bytes 786440 | tf_op jit(solution)/shard_map/ppermute | solution.py:205
  94.6 1.9 %collective-permute-start.8 = (bf16[4,128,256]{2,1,0:T(8,128)(2,1)}, bf16[4,128,256]{2,1,0:T(8,128)(2,1)S(1)}, u32[]{:S(2)}, u32[]{:S(2)}) collective-permute-start(bf16[4,128,256]{2,1,0:T(8,128)(2,1)} %get-tuple-element.49), channel_id=1, source_target_pairs={{5,0},{4,1},{7,2},{6,3},{1,4},{0,5},{3,6},{2,7},{13,8},{12,9},{15,... | collective-permute-start | bytes 786440 | tf_op jit(solution)/shard_map/ppermute | solution.py:205
  96.5 11.8 %all-to-all-start.1 = ((bf16[64,4,2,256]{3,2,1,0:T(2,128)(2,1)}), bf16[64,4,2,256]{3,2,1,0:T(2,128)(2,1)S(1)}, u32[]{:S(2)}, u32[]{:S(2)}) async-start(bf16[64,4,2,256]{3,2,1,0:T(2,128)(2,1)} %bitcast.16), calls=%async_computation.1 | async-start | bytes 524288 | tf_op jit(solution)/shard_map/all_to_all | solution.py:225
  108.3 5.1 %collective-permute-start.9 = (bf16[4,128,256]{2,1,0:T(8,128)(2,1)}, bf16[4,128,256]{2,1,0:T(8,128)(2,1)S(1)}, u32[]{:S(2)}, u32[]{:S(2)}) collective-permute-start(bf16[4,128,256]{2,1,0:T(8,128)(2,1)} %copy-done.8), channel_id=1, source_target_pairs={{2,0},{3,1},{4,2},{5,3},{6,4},{7,5},{0,6},{1,7},{10,8},{11,9},{12,... | collective-permute-start | bytes 786440 | tf_op jit(solution)/shard_map/ppermute | solution.py:205
  113.4 1.9 %collective-permute-start.10 = (bf16[4,128,256]{2,1,0:T(8,128)(2,1)}, bf16[4,128,256]{2,1,0:T(8,128)(2,1)S(1)}, u32[]{:S(2)}, u32[]{:S(2)}) collective-permute-start(bf16[4,128,256]{2,1,0:T(8,128)(2,1)} %copy-done.7), channel_id=1, source_target_pairs={{6,0},{7,1},{0,2},{1,3},{2,4},{3,5},{4,6},{5,7},{14,8},{15,9},{8,1... | collective-permute-start | bytes 786440 | tf_op jit(solution)/shard_map/ppermute | solution.py:205
  115.4 4.7 %collective-permute-start.11 = (bf16[4,128,256]{2,1,0:T(8,128)(2,1)}, bf16[4,128,256]{2,1,0:T(8,128)(2,1)S(1)}, u32[]{:S(2)}, u32[]{:S(2)}) collective-permute-start(bf16[4,128,256]{2,1,0:T(8,128)(2,1)} %copy-done.6), channel_id=1, source_target_pairs={{3,0},{2,1},{5,2},{4,3},{7,4},{6,5},{1,6},{0,7},{11,8},{10,9},{13,... | collective-permute-start | bytes 786440 | tf_op jit(solution)/shard_map/ppermute | solution.py:205
  120.0 0.0 collective-permute-done.7.refs_0_
  120.0 1.9 %collective-permute-start.12 = (bf16[4,128,256]{2,1,0:T(8,128)(2,1)S(1)}, bf16[4,128,256]{2,1,0:T(8,128)(2,1)S(1)}, u32[]{:S(2)}, u32[]{:S(2)}) collective-permute-start(bf16[4,128,256]{2,1,0:T(8,128)(2,1)S(1)} %get-tuple-element.53), channel_id=1, source_target_pairs={{7,0},{6,1},{1,2},{0,3},{3,4},{2,5},{5,6},{4,7},{15,8},{14,9},{9,1... | collective-permute-start | bytes 786440 | tf_op jit(solution)/shard_map/ppermute | solution.py:205
  122.0 0.0 collective-permute-done.8.refs_1_
  122.0 3.4 %collective-permute-start.13 = (bf16[4,128,256]{2,1,0:T(8,128)(2,1)S(1)}, bf16[4,128,256]{2,1,0:T(8,128)(2,1)S(1)}, u32[]{:S(2)}, u32[]{:S(2)}) collective-permute-start(bf16[4,128,256]{2,1,0:T(8,128)(2,1)S(1)} %get-tuple-element.54), channel_id=1, source_target_pairs={{1,0},{0,1},{3,2},{2,3},{5,4},{4,5},{7,6},{6,7},{9,8},{8,9},{11,10... | collective-permute-start | bytes 786440 | tf_op jit(solution)/shard_map/ppermute | solution.py:205
  125.4 0.0 collective-permute-done.9.refs_2_
  125.4 5.5 %collective-permute-done.10.refs_3_ = bf16[4,128,256]{2,1,0:T(8,128)(2,1)S(1)} collective-permute-done((bf16[4,128,256]{2,1,0:T(8,128)(2,1)}, bf16[4,128,256]{2,1,0:T(8,128)(2,1)S(1)}, u32[]{:S(2)}, u32[]{:S(2)}) %collective-permute-start.10) | collective-permute-done | bytes 262176 | tf_op jit(solution)/shard_map/ppermute | solution.py:205
  130.9 0.0 collective-permute-done.11.refs_4_
  130.9 11.6 %collective-permute-done.12.refs_5_ = bf16[4,128,256]{2,1,0:T(8,128)(2,1)S(1)} collective-permute-done((bf16[4,128,256]{2,1,0:T(8,128)(2,1)S(1)}, bf16[4,128,256]{2,1,0:T(8,128)(2,1)S(1)}, u32[]{:S(2)}, u32[]{:S(2)}) %collective-permute-start.12) | collective-permute-done | bytes 262176 | tf_op jit(solution)/shard_map/ppermute | solution.py:205
  142.6 0.0 collective-permute-done.13.refs_6_
  142.6 2.2 %unpack.1 = (bf16[128,2048]{1,0:T(8,128)(2,1)}, bf16[3,128,2048]{2,1,0:T(8,128)(2,1)}) custom-call(s32[2]{0:T(128)S(1)} %pad_add_fusion.place, bf16[4,128,256]{2,1,0:T(8,128)(2,1)S(1)} %collective-permute-done.7.refs_0_, bf16[4,128,256]{2,1,0:T(8,128)(2,1)S(1)} %collective-permute-done.8.refs_1_, bf16[4,128,256]{2,1,0:T(8,128)(2,1)S(1)} %collective-permute-done.9.refs_2_, ...), custom_call_target="tpu_custom_call" | custom-call | tf_op jit(solution)/shard_map/unpack/pallas_call | solution.py:187
  144.7 0.0 all-to-all-done.1
  144.7 0.7 copy.15
  (9 shorter events, 0.0 us)
Async XLA Ops:
  0.6 48.8 %copy-start = (bf16[256,256]{1,0:T(8,128)(2,1)S(1)}, bf16[256,256]{1,0:T(8,128)(2,1)}, u32[]{:S(2)}) copy-start(bf16[256,256]{1,0:T(8,128)(2,1)} %param.14) | copy-start | bytes 393220
  0.6 63.8 %copy-start.5 = (f32[128]{0:T(128)S(1)}, f32[128]{0:T(128)}, u32[]{:S(2)}) copy-start(f32[128]{0:T(128)} %param.17) | copy-start | bytes 1540
  0.7 63.8 %copy-start.4 = (f32[128]{0:T(128)S(1)}, f32[128]{0:T(128)}, u32[]{:S(2)}) copy-start(f32[128]{0:T(128)} %param.16) | copy-start | bytes 1540
  0.7 63.8 %copy-start.3 = (f32[128]{0:T(128)S(1)}, f32[128]{0:T(128)}, u32[]{:S(2)}) copy-start(f32[128]{0:T(128)} %param.15) | copy-start | bytes 1540
  0.8 1.4 copy-start.1
  2.2 1.0 copy-start.2
  4.9 36.4 %collective-permute-start = (bf16[4,128,256]{2,1,0:T(8,128)(2,1)S(1)}, bf16[4,128,256]{2,1,0:T(8,128)(2,1)S(1)}, u32[]{:S(2)}, u32[]{:S(2)}) collective-permute-start(bf16[4,128,256]{2,1,0:T(8,128)(2,1)S(1)} %get-tuple-element.40), channel_id=1, source_target_pairs={{0,4},{1,5},{2,6},{3,7},{4,0},{5,1},{6,2},{7,3},{8,12},{9,13},{10,... | collective-permute-start | bytes 786440 | tf_op jit(solution)/shard_map/ppermute | solution.py:205
  15.8 31.0 %collective-permute-start.1 = (bf16[4,128,256]{2,1,0:T(8,128)(2,1)S(1)}, bf16[4,128,256]{2,1,0:T(8,128)(2,1)S(1)}, u32[]{:S(2)}, u32[]{:S(2)}) collective-permute-start(bf16[4,128,256]{2,1,0:T(8,128)(2,1)S(1)} %get-tuple-element.41), channel_id=1, source_target_pairs={{0,5},{1,4},{2,7},{3,6},{4,1},{5,0},{6,3},{7,2},{8,13},{9,12},{10,... | collective-permute-start | bytes 786440 | tf_op jit(solution)/shard_map/ppermute | solution.py:205
  17.7 46.8 %all-to-all-start = ((bf16[64,4,2,256]{3,2,1,0:T(2,128)(2,1)}), bf16[64,4,2,256]{3,2,1,0:T(2,128)(2,1)S(1)}, u32[]{:S(2)}, u32[]{:S(2)}) async-start(bf16[64,4,2,256]{3,2,1,0:T(2,128)(2,1)} %param.10), calls=%async_computation | async-start | bytes 524288 | tf_op jit(solution)/shard_map/all_to_all | solution.py:217
  29.4 29.6 %collective-permute-start.2 = (bf16[4,128,256]{2,1,0:T(8,128)(2,1)}, bf16[4,128,256]{2,1,0:T(8,128)(2,1)S(1)}, u32[]{:S(2)}, u32[]{:S(2)}) collective-permute-start(bf16[4,128,256]{2,1,0:T(8,128)(2,1)} %get-tuple-element.42), channel_id=1, source_target_pairs={{0,2},{1,3},{2,4},{3,5},{4,6},{5,7},{6,0},{7,1},{8,10},{9,11},{10,... | collective-permute-start | bytes 786440 | tf_op jit(solution)/shard_map/ppermute | solution.py:205
  33.7 25.3 %collective-permute-start.3 = (bf16[4,128,256]{2,1,0:T(8,128)(2,1)}, bf16[4,128,256]{2,1,0:T(8,128)(2,1)S(1)}, u32[]{:S(2)}, u32[]{:S(2)}) collective-permute-start(bf16[4,128,256]{2,1,0:T(8,128)(2,1)} %get-tuple-element.43), channel_id=1, source_target_pairs={{0,6},{1,7},{2,0},{3,1},{4,2},{5,3},{6,4},{7,5},{8,14},{9,15},{10,... | collective-permute-start | bytes 786440 | tf_op jit(solution)/shard_map/ppermute | solution.py:205
  38.4 26.0 %collective-permute-start.4 = (bf16[4,128,256]{2,1,0:T(8,128)(2,1)S(1)}, bf16[4,128,256]{2,1,0:T(8,128)(2,1)S(1)}, u32[]{:S(2)}, u32[]{:S(2)}) collective-permute-start(bf16[4,128,256]{2,1,0:T(8,128)(2,1)S(1)} %get-tuple-element.44), channel_id=1, source_target_pairs={{0,3},{1,2},{2,5},{3,4},{4,7},{5,6},{6,1},{7,0},{8,11},{9,10},{10,... | collective-permute-start | bytes 786440 | tf_op jit(solution)/shard_map/ppermute | solution.py:205
  41.2 23.2 %collective-permute-start.5 = (bf16[4,128,256]{2,1,0:T(8,128)(2,1)S(1)}, bf16[4,128,256]{2,1,0:T(8,128)(2,1)S(1)}, u32[]{:S(2)}, u32[]{:S(2)}) collective-permute-start(bf16[4,128,256]{2,1,0:T(8,128)(2,1)S(1)} %get-tuple-element.45), channel_id=1, source_target_pairs={{0,7},{1,6},{2,1},{3,0},{4,3},{5,2},{6,5},{7,4},{8,15},{9,14},{10,... | collective-permute-start | bytes 786440 | tf_op jit(solution)/shard_map/ppermute | solution.py:205
  46.8 17.7 %collective-permute-start.6 = (bf16[4,128,256]{2,1,0:T(8,128)(2,1)S(1)}, bf16[4,128,256]{2,1,0:T(8,128)(2,1)S(1)}, u32[]{:S(2)}, u32[]{:S(2)}) collective-permute-start(bf16[4,128,256]{2,1,0:T(8,128)(2,1)S(1)} %get-tuple-element.46), channel_id=1, source_target_pairs={{0,1},{1,0},{2,3},{3,2},{4,5},{5,4},{6,7},{7,6},{8,9},{9,8},{10,11... | collective-permute-start | bytes 786440 | tf_op jit(solution)/shard_map/ppermute | solution.py:205
  85.2 0.7 copy-start.6
  85.9 0.7 copy-start.7
  86.6 0.7 copy-start.8
  87.3 32.7 %collective-permute-start.7 = (bf16[4,128,256]{2,1,0:T(8,128)(2,1)}, bf16[4,128,256]{2,1,0:T(8,128)(2,1)S(1)}, u32[]{:S(2)}, u32[]{:S(2)}) collective-permute-start(bf16[4,128,256]{2,1,0:T(8,128)(2,1)} %get-tuple-element.48), channel_id=1, source_target_pairs={{4,0},{5,1},{6,2},{7,3},{0,4},{1,5},{2,6},{3,7},{12,8},{13,9},{14,... | collective-permute-start | bytes 786440 | tf_op jit(solution)/shard_map/ppermute | solution.py:205
  94.6 27.4 %collective-permute-start.8 = (bf16[4,128,256]{2,1,0:T(8,128)(2,1)}, bf16[4,128,256]{2,1,0:T(8,128)(2,1)S(1)}, u32[]{:S(2)}, u32[]{:S(2)}) collective-permute-start(bf16[4,128,256]{2,1,0:T(8,128)(2,1)} %get-tuple-element.49), channel_id=1, source_target_pairs={{5,0},{4,1},{7,2},{6,3},{1,4},{0,5},{3,6},{2,7},{13,8},{12,9},{15,... | collective-permute-start | bytes 786440 | tf_op jit(solution)/shard_map/ppermute | solution.py:205
  96.5 48.2 %all-to-all-start.1 = ((bf16[64,4,2,256]{3,2,1,0:T(2,128)(2,1)}), bf16[64,4,2,256]{3,2,1,0:T(2,128)(2,1)S(1)}, u32[]{:S(2)}, u32[]{:S(2)}) async-start(bf16[64,4,2,256]{3,2,1,0:T(2,128)(2,1)} %bitcast.16), calls=%async_computation.1 | async-start | bytes 524288 | tf_op jit(solution)/shard_map/all_to_all | solution.py:225
  108.3 17.1 %collective-permute-start.9 = (bf16[4,128,256]{2,1,0:T(8,128)(2,1)}, bf16[4,128,256]{2,1,0:T(8,128)(2,1)S(1)}, u32[]{:S(2)}, u32[]{:S(2)}) collective-permute-start(bf16[4,128,256]{2,1,0:T(8,128)(2,1)} %copy-done.8), channel_id=1, source_target_pairs={{2,0},{3,1},{4,2},{5,3},{6,4},{7,5},{0,6},{1,7},{10,8},{11,9},{12,... | collective-permute-start | bytes 786440 | tf_op jit(solution)/shard_map/ppermute | solution.py:205
  113.4 17.5 %collective-permute-start.10 = (bf16[4,128,256]{2,1,0:T(8,128)(2,1)}, bf16[4,128,256]{2,1,0:T(8,128)(2,1)S(1)}, u32[]{:S(2)}, u32[]{:S(2)}) collective-permute-start(bf16[4,128,256]{2,1,0:T(8,128)(2,1)} %copy-done.7), channel_id=1, source_target_pairs={{6,0},{7,1},{0,2},{1,3},{2,4},{3,5},{4,6},{5,7},{14,8},{15,9},{8,1... | collective-permute-start | bytes 786440 | tf_op jit(solution)/shard_map/ppermute | solution.py:205
  115.4 15.6 %collective-permute-start.11 = (bf16[4,128,256]{2,1,0:T(8,128)(2,1)}, bf16[4,128,256]{2,1,0:T(8,128)(2,1)S(1)}, u32[]{:S(2)}, u32[]{:S(2)}) collective-permute-start(bf16[4,128,256]{2,1,0:T(8,128)(2,1)} %copy-done.6), channel_id=1, source_target_pairs={{3,0},{2,1},{5,2},{4,3},{7,4},{6,5},{1,6},{0,7},{11,8},{10,9},{13,... | collective-permute-start | bytes 786440 | tf_op jit(solution)/shard_map/ppermute | solution.py:205
  120.0 22.5 %collective-permute-start.12 = (bf16[4,128,256]{2,1,0:T(8,128)(2,1)S(1)}, bf16[4,128,256]{2,1,0:T(8,128)(2,1)S(1)}, u32[]{:S(2)}, u32[]{:S(2)}) collective-permute-start(bf16[4,128,256]{2,1,0:T(8,128)(2,1)S(1)} %get-tuple-element.53), channel_id=1, source_target_pairs={{7,0},{6,1},{1,2},{0,3},{3,4},{2,5},{5,6},{4,7},{15,8},{14,9},{9,1... | collective-permute-start | bytes 786440 | tf_op jit(solution)/shard_map/ppermute | solution.py:205
  122.0 20.6 %collective-permute-start.13 = (bf16[4,128,256]{2,1,0:T(8,128)(2,1)S(1)}, bf16[4,128,256]{2,1,0:T(8,128)(2,1)S(1)}, u32[]{:S(2)}, u32[]{:S(2)}) collective-permute-start(bf16[4,128,256]{2,1,0:T(8,128)(2,1)S(1)} %get-tuple-element.54), channel_id=1, source_target_pairs={{1,0},{0,1},{3,2},{2,3},{5,4},{4,5},{7,6},{6,7},{9,8},{8,9},{11,10... | collective-permute-start | bytes 786440 | tf_op jit(solution)/shard_map/ppermute | solution.py:205

commit v2 on v1

v2 whole, which is shorter than its diff:
```python
import functools
import math

import jax
import jax.numpy as jnp
from jax import lax
from jax.experimental import pallas as pl
from jax.experimental.pallas import tpu as pltpu
from jax.sharding import PartitionSpec as P

D = 2048
HEADS = 16
HS = D // HEADS
EPS = 1e-06
SCALE = 1.0 / math.sqrt(HS)
EXP2_SCALE = SCALE * math.log2(math.e)
CHIPS = 4
SEQ = 2 * CHIPS
OFFSETS = ((2, 0), (2, 1), (1, 0), (3, 0), (1, 1), (3, 1), (0, 1), (0, 0))
ROWS = 128
WIDTH = 256
HPD = WIDTH // HS
L = SEQ * ROWS
PROMPT = 256
KEYS = L + PROMPT
IN_PARTS, OUT_PARTS = 1, 1
IN_WIDTH, OUT_WIDTH = WIDTH // IN_PARTS, WIDTH // OUT_PARTS


def embedding(stamps, half_freq):
    frequency = jnp.exp(-math.log(10000.0) * jnp.arange(half_freq, dtype=jnp.float32) / half_freq)
    angles = stamps.astype(jnp.float32)[..., None] * frequency
    return jnp.concatenate([jnp.cos(angles), jnp.sin(angles)], axis=-1)


def normed(x, gain):
    r = lax.rsqrt(jnp.mean(x * x, axis=-1, keepdims=True) + EPS)
    return (x * r * gain).astype(jnp.bfloat16)


def norm_back(x, gain, upstream):
    r = lax.rsqrt(jnp.mean(x * x, axis=-1, keepdims=True) + EPS)
    weighted = upstream * gain
    along = jnp.mean(x * weighted, axis=-1, keepdims=True)
    return (weighted * r - x * (r * r * r * along)).astype(jnp.bfloat16)


def dot(a, b, dims):
    return lax.dot_general(a, b, (dims, ((), ())), preferred_element_type=jnp.float32)


NT = ((1,), (1,))
NN = ((1,), (0,))


def position():
    me = lax.axis_index("seq")
    return me // 2, me % 2


def partner(i, c, offset):
    dz, dc = offset
    return ((i + dz) % CHIPS) * 2 + (c + dc) % 2


def pack_kernel(place, img, cot, *outs):
    for h in range(IN_PARTS):
        for k, offset in enumerate(OFFSETS):
            out = outs[h * SEQ + k]
            d = partner(place[0], place[1], offset)
            columns = pl.ds(pl.multiple_of(d * WIDTH + h * IN_WIDTH, IN_WIDTH), IN_WIDTH)
            out[:3] = img[:, :, columns]
            out[3] = cot[:, columns]


def unpack_kernel(place, *refs):
    packed, (out, grads) = refs[:-2], refs[-2:]
    for h in range(OUT_PARTS):
        for k, offset in enumerate(OFFSETS):
            part = packed[h * SEQ + k]
            d = partner(place[0], place[1], offset)
            columns = pl.ds(pl.multiple_of(d * WIDTH + h * OUT_WIDTH, OUT_WIDTH), OUT_WIDTH)
            out[:, columns] = part[0]
            grads[:, :, columns] = part[1:]


def split_kernel(txt, tk, tv):
    tk[...] = txt[:, 0, :]
    tv[...] = txt[:, 1, :]


def attend_kernel(first, count, length, tk_ref, tv_ref, gate, gain_q, gain_k, gain_t, *refs):
    received, sent, (dtk, dtv) = refs[:SEQ], refs[SEQ : 2 * SEQ], refs[2 * SEQ : 2 * SEQ + 2]
    rin, rout, sems = refs[2 * SEQ + 2 :]
    start = 0 if received[0].shape[-1] == count * HS else first * HS
    copies = [
        pltpu.make_async_copy(r.at[:, :, pl.ds(start, count * HS)], rin.at[s], sems.at[s])
        for s, r in enumerate(received)
    ]
    for copy in copies:
        copy.start()
    for copy in copies:
        copy.wait()
    gq, gk, gt = gain_q[...], gain_k[...], gain_t[...]
    live = lax.broadcasted_iota(jnp.int32, (PROMPT, HS), 0) < length[0]
    lane = lax.broadcasted_iota(jnp.int32, (L, HS), 1)
    for h in range(count):
        columns = pl.ds(h * HS, HS)
        there = pl.ds((first + h) * HS, HS)
        gate_h = gate[:, there]
        q = rin[:, 0, :, columns].reshape(L, HS).astype(jnp.float32)
        k = rin[:, 1, :, columns].reshape(L, HS).astype(jnp.float32)
        v = rin[:, 2, :, columns].reshape(L, HS)
        cot = rin[:, 3, :, columns].reshape(L, HS).astype(jnp.float32)
        tk = tk_ref[:, there].astype(jnp.float32)
        tv = jnp.where(live, tv_ref[:, there].astype(jnp.float32), 0.0).astype(jnp.bfloat16)
        qn = normed(q, gq)
        kn = jnp.concatenate([normed(k, gk), normed(tk, gt)], axis=0)
        ones = jnp.concatenate(
            [jnp.ones((L, HS), jnp.bfloat16), jnp.where(live, 1.0, 0.0).astype(jnp.bfloat16)], axis=0
        )
        ve = jnp.concatenate([jnp.concatenate([v, tv], axis=0), ones], axis=1)
        e = jnp.exp2(dot(kn, qn, NT) * EXP2_SCALE)
        eb = e.astype(jnp.bfloat16)
        sums = dot(ve.T, eb, NN).T
        rz = 1.0 / sums[:, HS:]
        attn = sums[:, :HS] * rz
        rout[:, 0, :, columns] = (attn * gate_h).astype(jnp.bfloat16).reshape(SEQ, ROWS, HS)
        g = (cot * gate_h * rz).astype(jnp.bfloat16)
        delta = -jnp.sum(g.astype(jnp.float32) * attn, axis=-1, keepdims=True)
        hi = delta.astype(jnp.bfloat16).astype(jnp.float32)
        mid = (delta - hi).astype(jnp.bfloat16).astype(jnp.float32)
        low = delta - hi - mid
        tail = jnp.where(lane == 0, hi, jnp.where(lane == 1, mid, jnp.where(lane == 2, low, 0.0)))
        ge = jnp.concatenate([g, tail.astype(jnp.bfloat16)], axis=1)
        ds = (e * dot(ve, ge, NT)).astype(jnp.bfloat16)
        dv = dot(eb, g, NN)
        rout[:, 3, :, columns] = dv[:L].astype(jnp.bfloat16).reshape(SEQ, ROWS, HS)
        dtv[:, columns] = jnp.where(live, dv[L:], 0.0).astype(jnp.bfloat16)
        dk = dot(ds, qn, NN) * SCALE
        rout[:, 2, :, columns] = norm_back(k, gk, dk[:L]).reshape(SEQ, ROWS, HS)
        dtk[:, columns] = norm_back(tk, gt, dk[L:])
        dq = dot(kn.T, ds, NN).T * SCALE
        rout[:, 1, :, columns] = norm_back(q, gq, dq).reshape(SEQ, ROWS, HS)
    copies = [pltpu.make_async_copy(rout.at[s], r, sems.at[s]) for s, r in enumerate(sent)]
    for copy in copies:
        copy.start()
    for copy in copies:
        copy.wait()


def message(width):
    return jax.ShapeDtypeStruct((4, ROWS, width), jnp.bfloat16)


SMEM = pl.BlockSpec(memory_space=pltpu.SMEM)
VMEM = pl.BlockSpec(memory_space=pltpu.VMEM)
ANY = pl.BlockSpec(memory_space=pl.ANY)


def attend(first, count, length, tk, tv, gate, gain_q, gain_k, gain_t, received):
    width = count * HS
    prompt = jax.ShapeDtypeStruct((PROMPT, width), jnp.bfloat16)
    results = pl.pallas_call(
        functools.partial(attend_kernel, first, count),
        out_shape=[message(width)] * SEQ + [prompt] * 2,
        in_specs=[SMEM] + [VMEM] * 6 + [ANY] * SEQ,
        out_specs=[ANY] * SEQ + [VMEM] * 2,
        scratch_shapes=[
            pltpu.VMEM((SEQ, 4, ROWS, width), jnp.bfloat16),
            pltpu.VMEM((SEQ, 4, ROWS, width), jnp.bfloat16),
            pltpu.SemaphoreType.DMA((SEQ,)),
        ],
        compiler_params=pltpu.CompilerParams(vmem_limit_bytes=44 * 1024 * 1024),
        cost_estimate=pl.CostEstimate(
            flops=count * 12 * L * KEYS * HS, bytes_accessed=count * 4 * 1024 * 1024, transcendentals=count * L * KEYS
        ),
        name="attend",
    )(length, tk, tv, gate, gain_q, gain_k, gain_t, *received)
    return results[:SEQ], results[SEQ], results[SEQ + 1]


def pack(place, img, cot):
    return pl.pallas_call(
        pack_kernel,
        out_shape=[message(IN_WIDTH)] * (SEQ * IN_PARTS),
        in_specs=[SMEM, VMEM, VMEM],
        out_specs=[VMEM] * (SEQ * IN_PARTS),
        compiler_params=pltpu.CompilerParams(vmem_limit_bytes=16 * 1024 * 1024),
        name="pack",
    )(place, img, cot)


def split(txt):
    return pl.pallas_call(
        split_kernel,
        out_shape=[jax.ShapeDtypeStruct((PROMPT, WIDTH), jnp.bfloat16)] * 2,
        in_specs=[VMEM],
        out_specs=[VMEM] * 2,
        compiler_params=pltpu.CompilerParams(vmem_limit_bytes=8 * 1024 * 1024),
        name="split",
    )(txt)


def unpack(place, packed):
    return pl.pallas_call(
        unpack_kernel,
        out_shape=(
            jax.ShapeDtypeStruct((ROWS, D), jnp.bfloat16),
            jax.ShapeDtypeStruct((3, ROWS, D), jnp.bfloat16),
        ),
        in_specs=[SMEM] + [VMEM] * (SEQ * OUT_PARTS),
        out_specs=(VMEM, VMEM),
        compiler_params=pltpu.CompilerParams(vmem_limit_bytes=16 * 1024 * 1024),
        name="unpack",
    )(place, *packed)


def exchange(parts, way):
    results = []
    for offset, part in zip(OFFSETS * (len(parts) // SEQ), parts):
        if offset != (0, 0):
            pairs = [(me, partner(me // 2, me % 2, offset)) for me in range(SEQ)]
            part = lax.ppermute(part, "seq", pairs if way == 1 else [(b, a) for a, b in pairs])
        results.append(part)
    return results


def local(img_qkv, txt_kv, cot_img, timesteps, lengths, gate_w, gain_q, gain_k, gain_t):
    samples, text_rows = txt_kv.shape[:2]
    groups = ("grp", "fsdp")
    place = jnp.stack(position())
    messages = pack(place, img_qkv[0].transpose(1, 0, 2), cot_img[0])
    txt_kv, *messages = lax.optimization_barrier((txt_kv, *messages))
    received = exchange(messages, 1)
    prompt = lax.all_to_all(txt_kv, groups, split_axis=0, concat_axis=0, tiled=True)
    tk, tv = split(prompt.reshape(samples * text_rows, 2, WIDTH))
    embedded = embedding(timesteps, gate_w.shape[0] // 2)
    gate = jnp.dot(embedded, gate_w.astype(jnp.float32), precision=lax.Precision.HIGHEST)
    returned, d_prompt = [], []
    count = HPD // OUT_PARTS
    for p in range(OUT_PARTS):
        part = received[p * SEQ : (p + 1) * SEQ] if IN_PARTS > 1 else received
        sent, dtk, dtv = attend(
            p * count, count, lengths, tk, tv, gate, gain_q[None], gain_k[None], gain_t[None], part
        )
        returned += exchange(sent, -1)
        d_prompt.append(jnp.stack([dtk, dtv], axis=1))
    d_txt = jnp.concatenate(d_prompt, axis=-1).reshape(samples, text_rows, 2, WIDTH)
    d_txt = lax.all_to_all(d_txt, groups, split_axis=0, concat_axis=0, tiled=True)
    out, grads = unpack(place, returned)
    return out[None], grads.transpose(1, 0, 2)[None], d_txt


def solution(mesh):
    in_specs = (
        P(("grp", "fsdp"), "seq", None, None),
        P(None, ("grp", "fsdp"), None, "seq"),
        P(("grp", "fsdp"), "seq", None),
        P(("grp", "fsdp")),
        P(("grp", "fsdp")),
        P(None, "seq"),
        P(),
        P(),
        P(),
    )
    out_specs = (
        P(("grp", "fsdp"), "seq", None),
        P(("grp", "fsdp"), "seq", None, None),
        P(None, ("grp", "fsdp"), None, "seq"),
    )
    return jax.shard_map(local, mesh=mesh, in_specs=in_specs, out_specs=out_specs, check_vma=False)
```

time: 146 us -> 137 us (0.938)
  Pallas kernels: 24.4 us -> 14.7 us
  waiting for transfers between devices: 32 us -> 30.3 us
    pallas_call x2 -> x3, Pallas kernels: 22.3 us -> 12.5 us  [the longest x1 10.4 us: attend(): pl.pallas_call(functools.partial(attend_kernel, first, count), out_shape=...]
    ppermute x14, waiting for transfers between devices: 32 us -> 30.3 us  [exchange(): lax.ppermute(part, 'seq', pairs if way == 1 else [(b, a) for a, b in pairs])]
    unnamed x19 -> x21, local copies, waits for them, and re-layouts: 5.3 us -> 5.28 us
  transfers between devices with their start and end apart: 16 -> 16, of which waited for: 4 -> 5; matrix products, arithmetic and copies ran while one was open for 0% -> 1% of each run, Pallas kernels for 1% -> 2%
where the time goes in v2:
time: 137 us; the launch traced here: 135 us
  starting transfers between devices  81.2 us (59%)
  waiting for transfers between devices  30.3 us (22%)
  Pallas kernels  14.7 us (11%)
  local copies, waits for them, and re-layouts  5.38 us (4%)
  between operations  2.24 us (2%)
  other arithmetic  1.42 us (1%)
    ppermute x14, starting transfers between devices, exchange(): lax.ppermute(part, 'seq', pairs if way == 1 else [(b, a) for a, b in pairs])  57.8 us
    ppermute x14, waiting for transfers between devices, exchange(): lax.ppermute(part, 'seq', pairs if way == 1 else [(b, a) for a, b in pairs])  30.3 us
    all_to_all x1, starting transfers between devices, local(): lax.all_to_all(txt_kv, groups, split_axis=0, concat_axis=0, tiled=True)  11.7 us
    all_to_all x1, starting transfers between devices, local(): lax.all_to_all(d_txt, groups, split_axis=0, concat_axis=0, tiled=True)  11.7 us
    pallas_call x1, Pallas kernels, attend(): pl.pallas_call(functools.partial(attend_kernel, first, count), out_shape=...  10.4 us
    unnamed x21, local copies, waits for them, and re-layouts  5.28 us
  transfers between devices with their start and end apart: 16, of which 5 were waited for; matrix products, arithmetic and copies ran while one was open for 1% of the time, Pallas kernels for 2%

profile of v2, /device:TPU:6, one launch (start us, length us, event | category | flops | bytes accessed | tf_op | source)
XLA Modules:
  0.0 135.4 jit_solution(17053575569176656838)
XLA Ops:
  0.6 0.0 copy-start
  0.7 0.1 pad_add_fusion.place
  0.8 1.4 %copy-done.1 = bf16[1,128,3,2048]{3,1,2,0:T(8,128)(2,1)S(1)} copy-done((bf16[1,128,3,2048]{3,1,2,0:T(8,128)(2,1)S(1)}, bf16[1,128,3,2048]{3,1,2,0:T(8,128)(2,1)}, u32[]{:S(2)}) %copy-start.1) | copy-done | bytes 1572888
  2.2 1.0 copy-done.2
  3.2 1.5 %pack.1 = (bf16[4,128,256]{2,1,0:T(8,128)(2,1)}, bf16[4,128,256]{2,1,0:T(8,128)(2,1)S(1)}, bf16[4,128,256]{2,1,0:T(8,128)(2,1)S(1)}, bf16[4,128,256]{2,1,0:T(8,1...) custom-call(s32[2]{0:T(128)S(1)} %pad_add_fusion.place, ...), custom_call_target="tpu_custom_call" | custom-call | tf_op jit(solution)/shard_map/pack/pallas_call | solution.py:184
  4.8 10.9 %collective-permute-start = (bf16[4,128,256]{2,1,0:T(8,128)(2,1)}, bf16[4,128,256]{2,1,0:T(8,128)(2,1)S(1)}, u32[]{:S(2)}, u32[]{:S(2)}) collective-permute-start(bf16[4,128,256]{2,1,0:T(8,128)(2,1)} %get-tuple-element.45), channel_id=1, source_target_pairs={{0,4},{1,5},{2,6},{3,7},{4,0},{5,1},{6,2},{7,3},{8,12},{9,13},{10,... | collective-permute-start | bytes 786440 | tf_op jit(solution)/shard_map/ppermute | solution.py:224
  15.7 1.9 %collective-permute-start.1 = (bf16[4,128,256]{2,1,0:T(8,128)(2,1)S(1)}, bf16[4,128,256]{2,1,0:T(8,128)(2,1)S(1)}, u32[]{:S(2)}, u32[]{:S(2)}) collective-permute-start(bf16[4,128,256]{2,1,0:T(8,128)(2,1)S(1)} %get-tuple-element.46), channel_id=1, source_target_pairs={{0,5},{1,4},{2,7},{3,6},{4,1},{5,0},{6,3},{7,2},{8,13},{9,12},{10,... | collective-permute-start | bytes 786440 | tf_op jit(solution)/shard_map/ppermute | solution.py:224
  17.6 11.7 %all-to-all-start = ((bf16[64,4,2,256]{3,2,1,0:T(2,128)(2,1)}), bf16[64,4,2,256]{3,2,1,0:T(2,128)(2,1)S(1)}, u32[]{:S(2)}, u32[]{:S(2)}) async-start(bf16[64,4,2,256]{3,2,1,0:T(2,128)(2,1)} %param.10), calls=%async_computation | async-start | bytes 524288 | tf_op jit(solution)/shard_map/all_to_all | solution.py:236
  29.3 4.3 %collective-permute-start.2 = (bf16[4,128,256]{2,1,0:T(8,128)(2,1)S(1)}, bf16[4,128,256]{2,1,0:T(8,128)(2,1)S(1)}, u32[]{:S(2)}, u32[]{:S(2)}) collective-permute-start(bf16[4,128,256]{2,1,0:T(8,128)(2,1)S(1)} %get-tuple-element.47), channel_id=1, source_target_pairs={{0,2},{1,3},{2,4},{3,5},{4,6},{5,7},{6,0},{7,1},{8,10},{9,11},{10,... | collective-permute-start | bytes 786440 | tf_op jit(solution)/shard_map/ppermute | solution.py:224
  33.6 4.6 %collective-permute-start.3 = (bf16[4,128,256]{2,1,0:T(8,128)(2,1)S(1)}, bf16[4,128,256]{2,1,0:T(8,128)(2,1)S(1)}, u32[]{:S(2)}, u32[]{:S(2)}) collective-permute-start(bf16[4,128,256]{2,1,0:T(8,128)(2,1)S(1)} %get-tuple-element.48), channel_id=1, source_target_pairs={{0,6},{1,7},{2,0},{3,1},{4,2},{5,3},{6,4},{7,5},{8,14},{9,15},{10,... | collective-permute-start | bytes 786440 | tf_op jit(solution)/shard_map/ppermute | solution.py:224
  38.3 2.2 %collective-permute-start.4 = (bf16[4,128,256]{2,1,0:T(8,128)(2,1)S(1)}, bf16[4,128,256]{2,1,0:T(8,128)(2,1)S(1)}, u32[]{:S(2)}, u32[]{:S(2)}) collective-permute-start(bf16[4,128,256]{2,1,0:T(8,128)(2,1)S(1)} %get-tuple-element.49), channel_id=1, source_target_pairs={{0,3},{1,2},{2,5},{3,4},{4,7},{5,6},{6,1},{7,0},{8,11},{9,10},{10,... | collective-permute-start | bytes 786440 | tf_op jit(solution)/shard_map/ppermute | solution.py:224
  41.1 0.0 collective-permute-done.refs_0_
  41.2 5.5 %collective-permute-start.5 = (bf16[4,128,256]{2,1,0:T(8,128)(2,1)S(1)}, bf16[4,128,256]{2,1,0:T(8,128)(2,1)}, u32[]{:S(2)}, u32[]{:S(2)}) collective-permute-start(bf16[4,128,256]{2,1,0:T(8,128)(2,1)S(1)} %get-tuple-element.50), channel_id=1, source_target_pairs={{0,7},{1,6},{2,1},{3,0},{4,3},{5,2},{6,5},{7,4},{8,15},{9,14},{10,... | collective-permute-start | bytes 786440 | tf_op jit(solution)/shard_map/ppermute | solution.py:224
  46.6 0.0 collective-permute-done.1.refs_1_
  46.6 2.1 %collective-permute-start.6 = (bf16[4,128,256]{2,1,0:T(8,128)(2,1)S(1)}, bf16[4,128,256]{2,1,0:T(8,128)(2,1)}, u32[]{:S(2)}, u32[]{:S(2)}) collective-permute-start(bf16[4,128,256]{2,1,0:T(8,128)(2,1)S(1)} %get-tuple-element.51), channel_id=1, source_target_pairs={{0,1},{1,0},{2,3},{3,2},{4,5},{5,4},{6,7},{7,6},{8,9},{9,8},{10,11... | collective-permute-start | bytes 786440 | tf_op jit(solution)/shard_map/ppermute | solution.py:224
  48.7 0.1 fusion.3
  49.4 0.1 fusion.gate
  49.6 0.0 all-to-all-done
  49.6 0.6 split.1
  50.2 9.0 %collective-permute-done.2.refs_2_ = bf16[4,128,256]{2,1,0:T(8,128)(2,1)S(1)} collective-permute-done((bf16[4,128,256]{2,1,0:T(8,128)(2,1)S(1)}, bf16[4,128,256]{2,1,0:T(8,128)(2,1)S(1)}, u32[]{:S(2)}, u32[]{:S(2)}) %collective-permute-start.2) | collective-permute-done | bytes 262176 | tf_op jit(solution)/shard_map/ppermute | solution.py:224
  59.2 0.0 collective-permute-done.3.refs_3_
  59.2 5.5 %collective-permute-done.4.refs_4_ = bf16[4,128,256]{2,1,0:T(8,128)(2,1)S(1)} collective-permute-done((bf16[4,128,256]{2,1,0:T(8,128)(2,1)S(1)}, bf16[4,128,256]{2,1,0:T(8,128)(2,1)S(1)}, u32[]{:S(2)}, u32[]{:S(2)}) %collective-permute-start.4) | collective-permute-done | bytes 262176 | tf_op jit(solution)/shard_map/ppermute | solution.py:224
  64.7 0.0 collective-permute-done.5.refs_5_
  64.7 0.0 collective-permute-done.6.refs_6_
  64.7 10.4 %attend.1 = (bf16[4,128,256]{2,1,0:T(8,128)(2,1)S(1)}, bf16[4,128,256]{2,1,0:T(8,128)(2,1)S(1)}, bf16[4,128,256]{2,1,0:T(8,128)(2,1)S(1)}, bf16[4,128,256]{2,1,0...) custom-call(s32[1]{0:T(128)S(6)} %copy.16.length, ...), custom_call_target="tpu_custom_call" | custom-call | flops 4026531840 | bytes 8388608 | tf_op jit(solution)/shard_map/attend/pallas_call | solution.py:164
  75.1 0.0 copy-start.3
  75.1 0.7 copy-done.3
  75.8 0.7 copy-done.5
  76.5 0.7 copy-done.6
  77.3 7.2 %collective-permute-start.7 = (bf16[4,128,256]{2,1,0:T(8,128)(2,1)}, bf16[4,128,256]{2,1,0:T(8,128)(2,1)S(1)}, u32[]{:S(2)}, u32[]{:S(2)}) collective-permute-start(bf16[4,128,256]{2,1,0:T(8,128)(2,1)} %copy-done.6), channel_id=1, source_target_pairs={{4,0},{5,1},{6,2},{7,3},{0,4},{1,5},{2,6},{3,7},{12,8},{13,9},{14,... | collective-permute-start | bytes 786440 | tf_op jit(solution)/shard_map/ppermute | solution.py:224
  84.5 2.0 %collective-permute-start.8 = (bf16[4,128,256]{2,1,0:T(8,128)(2,1)}, bf16[4,128,256]{2,1,0:T(8,128)(2,1)S(1)}, u32[]{:S(2)}, u32[]{:S(2)}) collective-permute-start(bf16[4,128,256]{2,1,0:T(8,128)(2,1)} %copy-done.5), channel_id=1, source_target_pairs={{5,0},{4,1},{7,2},{6,3},{1,4},{0,5},{3,6},{2,7},{13,8},{12,9},{15,... | collective-permute-start | bytes 786440 | tf_op jit(solution)/shard_map/ppermute | solution.py:224
  86.5 1.3 pad_maximum_fusion
  87.8 11.7 %all-to-all-start.1 = ((bf16[64,4,2,256]{3,2,1,0:T(2,128)(2,1)}), bf16[64,4,2,256]{3,2,1,0:T(2,128)(2,1)S(1)}, u32[]{:S(2)}, u32[]{:S(2)}) async-start(bf16[64,4,2,256]{3,2,1,0:T(2,128)(2,1)} %pad_maximum_fusion), calls=%async_computation.1 | async-start | bytes 524288 | tf_op jit(solution)/shard_map/all_to_all | solution.py:250
  99.5 5.2 %collective-permute-start.9 = (bf16[4,128,256]{2,1,0:T(8,128)(2,1)S(1)}, bf16[4,128,256]{2,1,0:T(8,128)(2,1)S(1)}, u32[]{:S(2)}, u32[]{:S(2)}) collective-permute-start(bf16[4,128,256]{2,1,0:T(8,128)(2,1)S(1)} %copy-done.4), channel_id=1, source_target_pairs={{2,0},{3,1},{4,2},{5,3},{6,4},{7,5},{0,6},{1,7},{10,8},{11,9},{12,... | collective-permute-start | bytes 786440 | tf_op jit(solution)/shard_map/ppermute | solution.py:224
  104.7 1.9 %collective-permute-start.10 = (bf16[4,128,256]{2,1,0:T(8,128)(2,1)S(1)}, bf16[4,128,256]{2,1,0:T(8,128)(2,1)S(1)}, u32[]{:S(2)}, u32[]{:S(2)}) collective-permute-start(bf16[4,128,256]{2,1,0:T(8,128)(2,1)S(1)} %get-tuple-element.56), channel_id=1, source_target_pairs={{6,0},{7,1},{0,2},{1,3},{2,4},{3,5},{4,6},{5,7},{14,8},{15,9},{8,1... | collective-permute-start | bytes 786440 | tf_op jit(solution)/shard_map/ppermute | solution.py:224
  106.7 4.7 %collective-permute-start.11 = (bf16[4,128,256]{2,1,0:T(8,128)(2,1)S(1)}, bf16[4,128,256]{2,1,0:T(8,128)(2,1)S(1)}, u32[]{:S(2)}, u32[]{:S(2)}) collective-permute-start(bf16[4,128,256]{2,1,0:T(8,128)(2,1)S(1)} %get-tuple-element.57), channel_id=1, source_target_pairs={{3,0},{2,1},{5,2},{4,3},{7,4},{6,5},{1,6},{0,7},{11,8},{10,9},{13,... | collective-permute-start | bytes 786440 | tf_op jit(solution)/shard_map/ppermute | solution.py:224
  111.4 0.0 collective-permute-done.7.refs_0_
  111.4 1.9 %collective-permute-start.12 = (bf16[4,128,256]{2,1,0:T(8,128)(2,1)S(1)}, bf16[4,128,256]{2,1,0:T(8,128)(2,1)S(1)}, u32[]{:S(2)}, u32[]{:S(2)}) collective-permute-start(bf16[4,128,256]{2,1,0:T(8,128)(2,1)S(1)} %get-tuple-element.58), channel_id=1, source_target_pairs={{7,0},{6,1},{1,2},{0,3},{3,4},{2,5},{5,6},{4,7},{15,8},{14,9},{9,1... | collective-permute-start | bytes 786440 | tf_op jit(solution)/shard_map/ppermute | solution.py:224
  113.4 0.0 collective-permute-done.8.refs_1_
  113.4 3.3 %collective-permute-start.13 = (bf16[4,128,256]{2,1,0:T(8,128)(2,1)S(1)}, bf16[4,128,256]{2,1,0:T(8,128)(2,1)S(1)}, u32[]{:S(2)}, u32[]{:S(2)}) collective-permute-start(bf16[4,128,256]{2,1,0:T(8,128)(2,1)S(1)} %get-tuple-element.59), channel_id=1, source_target_pairs={{1,0},{0,1},{3,2},{2,3},{5,4},{4,5},{7,6},{6,7},{9,8},{8,9},{11,10... | collective-permute-start | bytes 786440 | tf_op jit(solution)/shard_map/ppermute | solution.py:224
  116.7 0.0 collective-permute-done.9.refs_2_
  116.7 3.1 %collective-permute-done.10.refs_3_ = bf16[4,128,256]{2,1,0:T(8,128)(2,1)S(1)} collective-permute-done((bf16[4,128,256]{2,1,0:T(8,128)(2,1)S(1)}, bf16[4,128,256]{2,1,0:T(8,128)(2,1)S(1)}, u32[]{:S(2)}, u32[]{:S(2)}) %collective-permute-start.10) | collective-permute-done | bytes 262176 | tf_op jit(solution)/shard_map/ppermute | solution.py:224
  119.8 0.5 collective-permute-done.11.refs_4_
  120.3 12.2 %collective-permute-done.12.refs_5_ = bf16[4,128,256]{2,1,0:T(8,128)(2,1)S(1)} collective-permute-done((bf16[4,128,256]{2,1,0:T(8,128)(2,1)S(1)}, bf16[4,128,256]{2,1,0:T(8,128)(2,1)S(1)}, u32[]{:S(2)}, u32[]{:S(2)}) %collective-permute-start.12) | collective-permute-done | bytes 262176 | tf_op jit(solution)/shard_map/ppermute | solution.py:224
  132.5 0.0 collective-permute-done.13.refs_6_
  132.5 2.2 %unpack.1 = (bf16[128,2048]{1,0:T(8,128)(2,1)}, bf16[3,128,2048]{2,1,0:T(8,128)(2,1)}) custom-call(s32[2]{0:T(128)S(1)} %pad_add_fusion.place, bf16[4,128,256]{2,1,0:T(8,128)(2,1)S(1)} %collective-permute-done.7.refs_0_, bf16[4,128,256]{2,1,0:T(8,128)(2,1)S(1)} %collective-permute-done.8.refs_1_, bf16[4,128,256]{2,1,0:T(8,128)(2,1)S(1)} %collective-permute-done.9.refs_2_, ...), custom_call_target="tpu_custom_call" | custom-call | tf_op jit(solution)/shard_map/unpack/pallas_call | solution.py:206
  134.7 0.0 all-to-all-done.1
  134.7 0.7 copy.17
  (15 shorter events, 0.1 us)
Async XLA Ops:
  0.6 48.8 %copy-start = (bf16[256,256]{1,0:T(8,128)(2,1)S(1)}, bf16[256,256]{1,0:T(8,128)(2,1)}, u32[]{:S(2)}) copy-start(bf16[256,256]{1,0:T(8,128)(2,1)} %param.14) | copy-start | bytes 393220
  0.6 64.0 %copy-start.9 = (f32[128]{0:T(128)S(1)}, f32[128]{0:T(128)}, u32[]{:S(2)}) copy-start(f32[128]{0:T(128)} %param.17) | copy-start | bytes 1540
  0.7 64.0 %copy-start.8 = (f32[128]{0:T(128)S(1)}, f32[128]{0:T(128)}, u32[]{:S(2)}) copy-start(f32[128]{0:T(128)} %param.16) | copy-start | bytes 1540
  0.7 64.0 %copy-start.7 = (f32[128]{0:T(128)S(1)}, f32[128]{0:T(128)}, u32[]{:S(2)}) copy-start(f32[128]{0:T(128)} %param.15) | copy-start | bytes 1540
  0.8 1.4 %copy-start.1 = (bf16[1,128,3,2048]{3,1,2,0:T(8,128)(2,1)S(1)}, bf16[1,128,3,2048]{3,1,2,0:T(8,128)(2,1)}, u32[]{:S(2)}) copy-start(bf16[1,128,3,2048]{3,1,2,0:T(8,128)(2,1)} %param.9) | copy-start | bytes 4718596
  2.2 1.0 copy-start.2
  4.8 36.4 %collective-permute-start = (bf16[4,128,256]{2,1,0:T(8,128)(2,1)}, bf16[4,128,256]{2,1,0:T(8,128)(2,1)S(1)}, u32[]{:S(2)}, u32[]{:S(2)}) collective-permute-start(bf16[4,128,256]{2,1,0:T(8,128)(2,1)} %get-tuple-element.45), channel_id=1, source_target_pairs={{0,4},{1,5},{2,6},{3,7},{4,0},{5,1},{6,2},{7,3},{8,12},{9,13},{10,... | collective-permute-start | bytes 786440 | tf_op jit(solution)/shard_map/ppermute | solution.py:224
  15.7 31.0 %collective-permute-start.1 = (bf16[4,128,256]{2,1,0:T(8,128)(2,1)S(1)}, bf16[4,128,256]{2,1,0:T(8,128)(2,1)S(1)}, u32[]{:S(2)}, u32[]{:S(2)}) collective-permute-start(bf16[4,128,256]{2,1,0:T(8,128)(2,1)S(1)} %get-tuple-element.46), channel_id=1, source_target_pairs={{0,5},{1,4},{2,7},{3,6},{4,1},{5,0},{6,3},{7,2},{8,13},{9,12},{10,... | collective-permute-start | bytes 786440 | tf_op jit(solution)/shard_map/ppermute | solution.py:224
  17.6 32.0 %all-to-all-start = ((bf16[64,4,2,256]{3,2,1,0:T(2,128)(2,1)}), bf16[64,4,2,256]{3,2,1,0:T(2,128)(2,1)S(1)}, u32[]{:S(2)}, u32[]{:S(2)}) async-start(bf16[64,4,2,256]{3,2,1,0:T(2,128)(2,1)} %param.10), calls=%async_computation | async-start | bytes 524288 | tf_op jit(solution)/shard_map/all_to_all | solution.py:236
  29.3 29.9 %collective-permute-start.2 = (bf16[4,128,256]{2,1,0:T(8,128)(2,1)S(1)}, bf16[4,128,256]{2,1,0:T(8,128)(2,1)S(1)}, u32[]{:S(2)}, u32[]{:S(2)}) collective-permute-start(bf16[4,128,256]{2,1,0:T(8,128)(2,1)S(1)} %get-tuple-element.47), channel_id=1, source_target_pairs={{0,2},{1,3},{2,4},{3,5},{4,6},{5,7},{6,0},{7,1},{8,10},{9,11},{10,... | collective-permute-start | bytes 786440 | tf_op jit(solution)/shard_map/ppermute | solution.py:224
  33.6 25.6 %collective-permute-start.3 = (bf16[4,128,256]{2,1,0:T(8,128)(2,1)S(1)}, bf16[4,128,256]{2,1,0:T(8,128)(2,1)S(1)}, u32[]{:S(2)}, u32[]{:S(2)}) collective-permute-start(bf16[4,128,256]{2,1,0:T(8,128)(2,1)S(1)} %get-tuple-element.48), channel_id=1, source_target_pairs={{0,6},{1,7},{2,0},{3,1},{4,2},{5,3},{6,4},{7,5},{8,14},{9,15},{10,... | collective-permute-start | bytes 786440 | tf_op jit(solution)/shard_map/ppermute | solution.py:224
  38.3 26.4 %collective-permute-start.4 = (bf16[4,128,256]{2,1,0:T(8,128)(2,1)S(1)}, bf16[4,128,256]{2,1,0:T(8,128)(2,1)S(1)}, u32[]{:S(2)}, u32[]{:S(2)}) collective-permute-start(bf16[4,128,256]{2,1,0:T(8,128)(2,1)S(1)} %get-tuple-element.49), channel_id=1, source_target_pairs={{0,3},{1,2},{2,5},{3,4},{4,7},{5,6},{6,1},{7,0},{8,11},{9,10},{10,... | collective-permute-start | bytes 786440 | tf_op jit(solution)/shard_map/ppermute | solution.py:224
  41.2 23.5 %collective-permute-start.5 = (bf16[4,128,256]{2,1,0:T(8,128)(2,1)S(1)}, bf16[4,128,256]{2,1,0:T(8,128)(2,1)}, u32[]{:S(2)}, u32[]{:S(2)}) collective-permute-start(bf16[4,128,256]{2,1,0:T(8,128)(2,1)S(1)} %get-tuple-element.50), channel_id=1, source_target_pairs={{0,7},{1,6},{2,1},{3,0},{4,3},{5,2},{6,5},{7,4},{8,15},{9,14},{10,... | collective-permute-start | bytes 786440 | tf_op jit(solution)/shard_map/ppermute | solution.py:224
  46.6 18.0 %collective-permute-start.6 = (bf16[4,128,256]{2,1,0:T(8,128)(2,1)S(1)}, bf16[4,128,256]{2,1,0:T(8,128)(2,1)}, u32[]{:S(2)}, u32[]{:S(2)}) collective-permute-start(bf16[4,128,256]{2,1,0:T(8,128)(2,1)S(1)} %get-tuple-element.51), channel_id=1, source_target_pairs={{0,1},{1,0},{2,3},{3,2},{4,5},{5,4},{6,7},{7,6},{8,9},{9,8},{10,11... | collective-permute-start | bytes 786440 | tf_op jit(solution)/shard_map/ppermute | solution.py:224
  75.1 0.7 copy-start.3
  75.8 0.7 copy-start.5
  76.5 0.7 copy-start.6
  77.2 22.3 %copy-start.4 = (bf16[4,128,256]{2,1,0:T(8,128)(2,1)S(1)}, bf16[4,128,256]{2,1,0:T(8,128)(2,1)}, u32[]{:S(2)}) copy-start(bf16[4,128,256]{2,1,0:T(8,128)(2,1)} %copy-done.3) | copy-start | bytes 786436
  77.3 34.1 %collective-permute-start.7 = (bf16[4,128,256]{2,1,0:T(8,128)(2,1)}, bf16[4,128,256]{2,1,0:T(8,128)(2,1)S(1)}, u32[]{:S(2)}, u32[]{:S(2)}) collective-permute-start(bf16[4,128,256]{2,1,0:T(8,128)(2,1)} %copy-done.6), channel_id=1, source_target_pairs={{4,0},{5,1},{6,2},{7,3},{0,4},{1,5},{2,6},{3,7},{12,8},{13,9},{14,... | collective-permute-start | bytes 786440 | tf_op jit(solution)/shard_map/ppermute | solution.py:224
  84.5 28.8 %collective-permute-start.8 = (bf16[4,128,256]{2,1,0:T(8,128)(2,1)}, bf16[4,128,256]{2,1,0:T(8,128)(2,1)S(1)}, u32[]{:S(2)}, u32[]{:S(2)}) collective-permute-start(bf16[4,128,256]{2,1,0:T(8,128)(2,1)} %copy-done.5), channel_id=1, source_target_pairs={{5,0},{4,1},{7,2},{6,3},{1,4},{0,5},{3,6},{2,7},{13,8},{12,9},{15,... | collective-permute-start | bytes 786440 | tf_op jit(solution)/shard_map/ppermute | solution.py:224
  87.8 46.9 %all-to-all-start.1 = ((bf16[64,4,2,256]{3,2,1,0:T(2,128)(2,1)}), bf16[64,4,2,256]{3,2,1,0:T(2,128)(2,1)S(1)}, u32[]{:S(2)}, u32[]{:S(2)}) async-start(bf16[64,4,2,256]{3,2,1,0:T(2,128)(2,1)} %pad_maximum_fusion), calls=%async_computation.1 | async-start | bytes 524288 | tf_op jit(solution)/shard_map/all_to_all | solution.py:250
  99.5 17.2 %collective-permute-start.9 = (bf16[4,128,256]{2,1,0:T(8,128)(2,1)S(1)}, bf16[4,128,256]{2,1,0:T(8,128)(2,1)S(1)}, u32[]{:S(2)}, u32[]{:S(2)}) collective-permute-start(bf16[4,128,256]{2,1,0:T(8,128)(2,1)S(1)} %copy-done.4), channel_id=1, source_target_pairs={{2,0},{3,1},{4,2},{5,3},{6,4},{7,5},{0,6},{1,7},{10,8},{11,9},{12,... | collective-permute-start | bytes 786440 | tf_op jit(solution)/shard_map/ppermute | solution.py:224
  104.7 15.1 %collective-permute-start.10 = (bf16[4,128,256]{2,1,0:T(8,128)(2,1)S(1)}, bf16[4,128,256]{2,1,0:T(8,128)(2,1)S(1)}, u32[]{:S(2)}, u32[]{:S(2)}) collective-permute-start(bf16[4,128,256]{2,1,0:T(8,128)(2,1)S(1)} %get-tuple-element.56), channel_id=1, source_target_pairs={{6,0},{7,1},{0,2},{1,3},{2,4},{3,5},{4,6},{5,7},{14,8},{15,9},{8,1... | collective-permute-start | bytes 786440 | tf_op jit(solution)/shard_map/ppermute | solution.py:224
  106.7 13.7 %collective-permute-start.11 = (bf16[4,128,256]{2,1,0:T(8,128)(2,1)S(1)}, bf16[4,128,256]{2,1,0:T(8,128)(2,1)S(1)}, u32[]{:S(2)}, u32[]{:S(2)}) collective-permute-start(bf16[4,128,256]{2,1,0:T(8,128)(2,1)S(1)} %get-tuple-element.57), channel_id=1, source_target_pairs={{3,0},{2,1},{5,2},{4,3},{7,4},{6,5},{1,6},{0,7},{11,8},{10,9},{13,... | collective-permute-start | bytes 786440 | tf_op jit(solution)/shard_map/ppermute | solution.py:224
  111.4 21.1 %collective-permute-start.12 = (bf16[4,128,256]{2,1,0:T(8,128)(2,1)S(1)}, bf16[4,128,256]{2,1,0:T(8,128)(2,1)S(1)}, u32[]{:S(2)}, u32[]{:S(2)}) collective-permute-start(bf16[4,128,256]{2,1,0:T(8,128)(2,1)S(1)} %get-tuple-element.58), channel_id=1, source_target_pairs={{7,0},{6,1},{1,2},{0,3},{3,4},{2,5},{5,6},{4,7},{15,8},{14,9},{9,1... | collective-permute-start | bytes 786440 | tf_op jit(solution)/shard_map/ppermute | solution.py:224
  113.4 19.2 %collective-permute-start.13 = (bf16[4,128,256]{2,1,0:T(8,128)(2,1)S(1)}, bf16[4,128,256]{2,1,0:T(8,128)(2,1)S(1)}, u32[]{:S(2)}, u32[]{:S(2)}) collective-permute-start(bf16[4,128,256]{2,1,0:T(8,128)(2,1)S(1)} %get-tuple-element.59), channel_id=1, source_target_pairs={{1,0},{0,1},{3,2},{2,3},{5,4},{4,5},{7,6},{6,7},{9,8},{8,9},{11,10... | collective-permute-start | bytes 786440 | tf_op jit(solution)/shard_map/ppermute | solution.py:224

commit v3 on v2

--- a/solution.py
+++ b/solution.py
@@ -89,29 +89,33 @@
     tv[...] = txt[:, 1, :]
 
 
+def merge_kernel(dtk, dtv, d_txt):
+    d_txt[:, 0, :] = dtk[...]
+    d_txt[:, 1, :] = dtv[...]
+
+
 def attend_kernel(first, count, length, tk_ref, tv_ref, gate, gain_q, gain_k, gain_t, *refs):
-    received, sent, (dtk, dtv) = refs[:SEQ], refs[SEQ : 2 * SEQ], refs[2 * SEQ : 2 * SEQ + 2]
-    rin, rout, sems = refs[2 * SEQ + 2 :]
+    received, sent, (dtk, dtv) = refs[:SEQ], refs[SEQ : 2 * SEQ], refs[2 * SEQ :]
     start = 0 if received[0].shape[-1] == count * HS else first * HS
-    copies = [
-        pltpu.make_async_copy(r.at[:, :, pl.ds(start, count * HS)], rin.at[s], sems.at[s])
-        for s, r in enumerate(received)
-    ]
-    for copy in copies:
-        copy.start()
-    for copy in copies:
-        copy.wait()
     gq, gk, gt = gain_q[...], gain_k[...], gain_t[...]
     live = lax.broadcasted_iota(jnp.int32, (PROMPT, HS), 0) < length[0]
     lane = lax.broadcasted_iota(jnp.int32, (L, HS), 1)
-    for h in range(count):
+
+    def gather(a, h):
+        return jnp.concatenate([r[a, :, pl.ds(start + h * HS, HS)] for r in received], axis=0)
+
+    def scatter(a, h, values):
+        for s, r in enumerate(sent):
+            r[a, :, pl.ds(h * HS, HS)] = values[s * ROWS : (s + 1) * ROWS]
+
+    def head(h):
         columns = pl.ds(h * HS, HS)
         there = pl.ds((first + h) * HS, HS)
         gate_h = gate[:, there]
-        q = rin[:, 0, :, columns].reshape(L, HS).astype(jnp.float32)
-        k = rin[:, 1, :, columns].reshape(L, HS).astype(jnp.float32)
-        v = rin[:, 2, :, columns].reshape(L, HS)
-        cot = rin[:, 3, :, columns].reshape(L, HS).astype(jnp.float32)
+        q = gather(0, h).astype(jnp.float32)
+        k = gather(1, h).astype(jnp.float32)
+        v = gather(2, h)
+        cot = gather(3, h).astype(jnp.float32)
         tk = tk_ref[:, there].astype(jnp.float32)
         tv = jnp.where(live, tv_ref[:, there].astype(jnp.float32), 0.0).astype(jnp.bfloat16)
         qn = normed(q, gq)
@@ -122,10 +126,12 @@
         ve = jnp.concatenate([jnp.concatenate([v, tv], axis=0), ones], axis=1)
         e = jnp.exp2(dot(kn, qn, NT) * EXP2_SCALE)
         eb = e.astype(jnp.bfloat16)
+        yield
         sums = dot(ve.T, eb, NN).T
+        yield
         rz = 1.0 / sums[:, HS:]
         attn = sums[:, :HS] * rz
-        rout[:, 0, :, columns] = (attn * gate_h).astype(jnp.bfloat16).reshape(SEQ, ROWS, HS)
+        scatter(0, h, (attn * gate_h).astype(jnp.bfloat16))
         g = (cot * gate_h * rz).astype(jnp.bfloat16)
         delta = -jnp.sum(g.astype(jnp.float32) * attn, axis=-1, keepdims=True)
         hi = delta.astype(jnp.bfloat16).astype(jnp.float32)
@@ -133,20 +139,25 @@
         low = delta - hi - mid
         tail = jnp.where(lane == 0, hi, jnp.where(lane == 1, mid, jnp.where(lane == 2, low, 0.0)))
         ge = jnp.concatenate([g, tail.astype(jnp.bfloat16)], axis=1)
+        yield
         ds = (e * dot(ve, ge, NT)).astype(jnp.bfloat16)
+        yield
         dv = dot(eb, g, NN)
-        rout[:, 3, :, columns] = dv[:L].astype(jnp.bfloat16).reshape(SEQ, ROWS, HS)
+        yield
+        scatter(3, h, dv[:L].astype(jnp.bfloat16))
         dtv[:, columns] = jnp.where(live, dv[L:], 0.0).astype(jnp.bfloat16)
         dk = dot(ds, qn, NN) * SCALE
-        rout[:, 2, :, columns] = norm_back(k, gk, dk[:L]).reshape(SEQ, ROWS, HS)
+        yield
+        scatter(2, h, norm_back(k, gk, dk[:L]))
         dtk[:, columns] = norm_back(tk, gt, dk[L:])
         dq = dot(kn.T, ds, NN).T * SCALE
-        rout[:, 1, :, columns] = norm_back(q, gq, dq).reshape(SEQ, ROWS, HS)
-    copies = [pltpu.make_async_copy(rout.at[s], r, sems.at[s]) for s, r in enumerate(sent)]
-    for copy in copies:
-        copy.start()
-    for copy in copies:
-        copy.wait()
+        scatter(1, h, norm_back(q, gq, dq))
+        yield
+
+    heads = [head(h) for h in range(count)]
+    next(heads[0])
+    while heads:
+        heads = [g for g in heads if next(g, heads) is not heads]
 
 
 def message(width):
@@ -164,13 +175,8 @@
     results = pl.pallas_call(
         functools.partial(attend_kernel, first, count),
         out_shape=[message(width)] * SEQ + [prompt] * 2,
-        in_specs=[SMEM] + [VMEM] * 6 + [ANY] * SEQ,
-        out_specs=[ANY] * SEQ + [VMEM] * 2,
-        scratch_shapes=[
-            pltpu.VMEM((SEQ, 4, ROWS, width), jnp.bfloat16),
-            pltpu.VMEM((SEQ, 4, ROWS, width), jnp.bfloat16),
-            pltpu.SemaphoreType.DMA((SEQ,)),
-        ],
+        in_specs=[SMEM] + [VMEM] * (6 + SEQ),
+        out_specs=[VMEM] * (SEQ + 2),
         compiler_params=pltpu.CompilerParams(vmem_limit_bytes=44 * 1024 * 1024),
         cost_estimate=pl.CostEstimate(
             flops=count * 12 * L * KEYS * HS, bytes_accessed=count * 4 * 1024 * 1024, transcendentals=count * L * KEYS
@@ -200,6 +206,17 @@
         compiler_params=pltpu.CompilerParams(vmem_limit_bytes=8 * 1024 * 1024),
         name="split",
     )(txt)
+
+
+def merge(dtk, dtv):
+    return pl.pallas_call(
+        merge_kernel,
+        out_shape=jax.ShapeDtypeStruct((PROMPT, 2, WIDTH), jnp.bfloat16),
+        in_specs=[VMEM] * 2,
+        out_specs=VMEM,
+        compiler_params=pltpu.CompilerParams(vmem_limit_bytes=8 * 1024 * 1024),
+        name="merge",
+    )(dtk, dtv)
 
 
 def unpack(place, packed):
@@ -245,7 +262,7 @@
             p * count, count, lengths, tk, tv, gate, gain_q[None], gain_k[None], gain_t[None], part
         )
         returned += exchange(sent, -1)
-        d_prompt.append(jnp.stack([dtk, dtv], axis=1))
+        d_prompt.append(merge(dtk, dtv))
     d_txt = jnp.concatenate(d_prompt, axis=-1).reshape(samples, text_rows, 2, WIDTH)
     d_txt = lax.all_to_all(d_txt, groups, split_axis=0, concat_axis=0, tiled=True)
     out, grads = unpack(place, returned)

time: 137 us -> 134 us (0.978)
  local copies, waits for them, and re-layouts: 5.38 us -> 3.17 us
    unnamed x21 -> x13, local copies, waits for them, and re-layouts: 5.28 us -> 3.17 us
  transfers between devices with their start and end apart: 16 -> 16, of which waited for: 5 -> 4; matrix products, arithmetic and copies ran while one was open for 1% -> 0% of each run, Pallas kernels for 2% -> 3%
where the time goes in v3:
time: 134 us; the launch traced here: 133 us
  starting transfers between devices  81.3 us (61%)
  waiting for transfers between devices  30.3 us (23%)
  Pallas kernels  15.5 us (12%)
  local copies, waits for them, and re-layouts  3.17 us (2%)
  between operations  2.2 us (2%)
    ppermute x14, starting transfers between devices, exchange(): lax.ppermute(part, 'seq', pairs if way == 1 else [(b, a) for a, b in pairs])  57.8 us
    ppermute x14, waiting for transfers between devices, exchange(): lax.ppermute(part, 'seq', pairs if way == 1 else [(b, a) for a, b in pairs])  30.3 us
    all_to_all x1, starting transfers between devices, local(): lax.all_to_all(d_txt, groups, split_axis=0, concat_axis=0, tiled=True)  11.8 us
    all_to_all x1, starting transfers between devices, local(): lax.all_to_all(txt_kv, groups, split_axis=0, concat_axis=0, tiled=True)  11.7 us
    pallas_call x1, Pallas kernels, attend(): pl.pallas_call(functools.partial(attend_kernel, first, count), out_shape=...  9.96 us
    unnamed x13, local copies, waits for them, and re-layouts  3.17 us
  transfers between devices with their start and end apart: 16, of which 4 were waited for; matrix products, arithmetic and copies ran while one was open for 0% of the time, Pallas kernels for 3%

profile of v3, /device:TPU:6, one launch (start us, length us, event | category | flops | bytes accessed | tf_op | source)
XLA Modules:
  0.0 132.7 jit_solution(73550068886566086)
XLA Ops:
  0.6 0.0 copy-start
  0.6 0.0 copy-start.5
  0.7 0.0 copy-start.4
  0.7 0.1 pad_add_fusion.place
  0.8 1.4 %copy-done.1 = bf16[1,128,3,2048]{3,1,2,0:T(8,128)(2,1)S(1)} copy-done((bf16[1,128,3,2048]{3,1,2,0:T(8,128)(2,1)S(1)}, bf16[1,128,3,2048]{3,1,2,0:T(8,128)(2,1)}, u32[]{:S(2)}) %copy-start.1) | copy-done | bytes 1572888
  2.2 1.0 copy-done.2
  3.2 1.6 %pack.1 = (bf16[4,128,256]{2,1,0:T(8,128)(2,1)}, bf16[4,128,256]{2,1,0:T(8,128)(2,1)}, bf16[4,128,256]{2,1,0:T(8,128)(2,1)S(1)}, bf16[4,128,256]{2,1,0:T(8,128)(...) custom-call(s32[2]{0:T(128)S(1)} %pad_add_fusion.place, ...), custom_call_target="tpu_custom_call" | custom-call | tf_op jit(solution)/shard_map/pack/pallas_call | solution.py:190
  4.9 10.9 %collective-permute-start = (bf16[4,128,256]{2,1,0:T(8,128)(2,1)}, bf16[4,128,256]{2,1,0:T(8,128)(2,1)S(1)}, u32[]{:S(2)}, u32[]{:S(2)}) collective-permute-start(bf16[4,128,256]{2,1,0:T(8,128)(2,1)} %get-tuple-element.45), channel_id=1, source_target_pairs={{0,4},{1,5},{2,6},{3,7},{4,0},{5,1},{6,2},{7,3},{8,12},{9,13},{10,... | collective-permute-start | bytes 786440 | tf_op jit(solution)/shard_map/ppermute | solution.py:241
  15.8 1.9 %collective-permute-start.1 = (bf16[4,128,256]{2,1,0:T(8,128)(2,1)}, bf16[4,128,256]{2,1,0:T(8,128)(2,1)S(1)}, u32[]{:S(2)}, u32[]{:S(2)}) collective-permute-start(bf16[4,128,256]{2,1,0:T(8,128)(2,1)} %get-tuple-element.46), channel_id=1, source_target_pairs={{0,5},{1,4},{2,7},{3,6},{4,1},{5,0},{6,3},{7,2},{8,13},{9,12},{10,... | collective-permute-start | bytes 786440 | tf_op jit(solution)/shard_map/ppermute | solution.py:241
  17.7 11.7 %all-to-all-start = ((bf16[64,4,2,256]{3,2,1,0:T(2,128)(2,1)}), bf16[64,4,2,256]{3,2,1,0:T(2,128)(2,1)S(1)}, u32[]{:S(2)}, u32[]{:S(2)}) async-start(bf16[64,4,2,256]{3,2,1,0:T(2,128)(2,1)} %param.10), calls=%async_computation | async-start | bytes 524288 | tf_op jit(solution)/shard_map/all_to_all | solution.py:253
  29.4 4.3 %collective-permute-start.2 = (bf16[4,128,256]{2,1,0:T(8,128)(2,1)S(1)}, bf16[4,128,256]{2,1,0:T(8,128)(2,1)S(1)}, u32[]{:S(2)}, u32[]{:S(2)}) collective-permute-start(bf16[4,128,256]{2,1,0:T(8,128)(2,1)S(1)} %get-tuple-element.47), channel_id=1, source_target_pairs={{0,2},{1,3},{2,4},{3,5},{4,6},{5,7},{6,0},{7,1},{8,10},{9,11},{10,... | collective-permute-start | bytes 786440 | tf_op jit(solution)/shard_map/ppermute | solution.py:241
  33.7 4.6 %collective-permute-start.3 = (bf16[4,128,256]{2,1,0:T(8,128)(2,1)S(1)}, bf16[4,128,256]{2,1,0:T(8,128)(2,1)S(1)}, u32[]{:S(2)}, u32[]{:S(2)}) collective-permute-start(bf16[4,128,256]{2,1,0:T(8,128)(2,1)S(1)} %get-tuple-element.48), channel_id=1, source_target_pairs={{0,6},{1,7},{2,0},{3,1},{4,2},{5,3},{6,4},{7,5},{8,14},{9,15},{10,... | collective-permute-start | bytes 786440 | tf_op jit(solution)/shard_map/ppermute | solution.py:241
  38.4 2.2 %collective-permute-start.4 = (bf16[4,128,256]{2,1,0:T(8,128)(2,1)S(1)}, bf16[4,128,256]{2,1,0:T(8,128)(2,1)S(1)}, u32[]{:S(2)}, u32[]{:S(2)}) collective-permute-start(bf16[4,128,256]{2,1,0:T(8,128)(2,1)S(1)} %get-tuple-element.49), channel_id=1, source_target_pairs={{0,3},{1,2},{2,5},{3,4},{4,7},{5,6},{6,1},{7,0},{8,11},{9,10},{10,... | collective-permute-start | bytes 786440 | tf_op jit(solution)/shard_map/ppermute | solution.py:241
  41.2 0.0 collective-permute-done.refs_0_
  41.2 5.5 %collective-permute-start.5 = (bf16[4,128,256]{2,1,0:T(8,128)(2,1)S(1)}, bf16[4,128,256]{2,1,0:T(8,128)(2,1)}, u32[]{:S(2)}, u32[]{:S(2)}) collective-permute-start(bf16[4,128,256]{2,1,0:T(8,128)(2,1)S(1)} %get-tuple-element.50), channel_id=1, source_target_pairs={{0,7},{1,6},{2,1},{3,0},{4,3},{5,2},{6,5},{7,4},{8,15},{9,14},{10,... | collective-permute-start | bytes 786440 | tf_op jit(solution)/shard_map/ppermute | solution.py:241
  46.7 0.0 collective-permute-done.1.refs_1_
  46.7 2.1 %collective-permute-start.6 = (bf16[4,128,256]{2,1,0:T(8,128)(2,1)S(1)}, bf16[4,128,256]{2,1,0:T(8,128)(2,1)}, u32[]{:S(2)}, u32[]{:S(2)}) collective-permute-start(bf16[4,128,256]{2,1,0:T(8,128)(2,1)S(1)} %get-tuple-element.51), channel_id=1, source_target_pairs={{0,1},{1,0},{2,3},{3,2},{4,5},{5,4},{6,7},{7,6},{8,9},{9,8},{10,11... | collective-permute-start | bytes 786440 | tf_op jit(solution)/shard_map/ppermute | solution.py:241
  48.8 0.1 fusion.3
  49.5 0.1 fusion.gate
  49.7 0.0 all-to-all-done
  49.7 0.6 split.1
  50.3 8.9 %collective-permute-done.2.refs_2_ = bf16[4,128,256]{2,1,0:T(8,128)(2,1)S(1)} collective-permute-done((bf16[4,128,256]{2,1,0:T(8,128)(2,1)S(1)}, bf16[4,128,256]{2,1,0:T(8,128)(2,1)S(1)}, u32[]{:S(2)}, u32[]{:S(2)}) %collective-permute-start.2) | collective-permute-done | bytes 262176 | tf_op jit(solution)/shard_map/ppermute | solution.py:241
  59.2 0.0 collective-permute-done.3.refs_3_
  59.2 5.5 %collective-permute-done.4.refs_4_ = bf16[4,128,256]{2,1,0:T(8,128)(2,1)S(1)} collective-permute-done((bf16[4,128,256]{2,1,0:T(8,128)(2,1)S(1)}, bf16[4,128,256]{2,1,0:T(8,128)(2,1)S(1)}, u32[]{:S(2)}, u32[]{:S(2)}) %collective-permute-start.4) | collective-permute-done | bytes 262176 | tf_op jit(solution)/shard_map/ppermute | solution.py:241
  64.7 0.0 collective-permute-done.5.refs_5_
  64.7 0.0 collective-permute-done.6.refs_6_
  64.7 0.0 copy-done.4
  64.7 0.0 copy-done.3
  64.7 10.0 %attend.1 = (bf16[4,128,256]{2,1,0:T(8,128)(2,1)}, bf16[4,128,256]{2,1,0:T(8,128)(2,1)}, bf16[4,128,256]{2,1,0:T(8,128)(2,1)S(1)}, bf16[4,128,256]{2,1,0:T(8,128...) custom-call(s32[1]{0:T(128)S(6)} %copy.14.length, ...), custom_call_target="tpu_custom_call" | custom-call | flops 4026531840 | bytes 8388608 | tf_op jit(solution)/shard_map/attend/pallas_call | solution.py:175
  74.7 7.2 %collective-permute-start.7 = (bf16[4,128,256]{2,1,0:T(8,128)(2,1)}, bf16[4,128,256]{2,1,0:T(8,128)(2,1)S(1)}, u32[]{:S(2)}, u32[]{:S(2)}) collective-permute-start(bf16[4,128,256]{2,1,0:T(8,128)(2,1)} %get-tuple-element.53), channel_id=1, source_target_pairs={{4,0},{5,1},{6,2},{7,3},{0,4},{1,5},{2,6},{3,7},{12,8},{13,9},{14,... | collective-permute-start | bytes 786440 | tf_op jit(solution)/shard_map/ppermute | solution.py:241
  81.8 2.0 %collective-permute-start.8 = (bf16[4,128,256]{2,1,0:T(8,128)(2,1)}, bf16[4,128,256]{2,1,0:T(8,128)(2,1)S(1)}, u32[]{:S(2)}, u32[]{:S(2)}) collective-permute-start(bf16[4,128,256]{2,1,0:T(8,128)(2,1)} %get-tuple-element.54), channel_id=1, source_target_pairs={{5,0},{4,1},{7,2},{6,3},{1,4},{0,5},{3,6},{2,7},{13,8},{12,9},{15,... | collective-permute-start | bytes 786440 | tf_op jit(solution)/shard_map/ppermute | solution.py:241
  83.9 1.2 merge.1
  85.0 11.8 %all-to-all-start.1 = ((bf16[64,4,2,256]{3,2,1,0:T(2,128)(2,1)}), bf16[64,4,2,256]{3,2,1,0:T(2,128)(2,1)S(1)}, u32[]{:S(2)}, u32[]{:S(2)}) async-start(bf16[64,4,2,256]{3,2,1,0:T(2,128)(2,1)} %bitcast.16), calls=%async_computation.1 | async-start | bytes 524288 | tf_op jit(solution)/shard_map/all_to_all | solution.py:267
  96.9 5.2 %collective-permute-start.9 = (bf16[4,128,256]{2,1,0:T(8,128)(2,1)S(1)}, bf16[4,128,256]{2,1,0:T(8,128)(2,1)S(1)}, u32[]{:S(2)}, u32[]{:S(2)}) collective-permute-start(bf16[4,128,256]{2,1,0:T(8,128)(2,1)S(1)} %get-tuple-element.55), channel_id=1, source_target_pairs={{2,0},{3,1},{4,2},{5,3},{6,4},{7,5},{0,6},{1,7},{10,8},{11,9},{12,... | collective-permute-start | bytes 786440 | tf_op jit(solution)/shard_map/ppermute | solution.py:241
  102.0 1.9 %collective-permute-start.10 = (bf16[4,128,256]{2,1,0:T(8,128)(2,1)S(1)}, bf16[4,128,256]{2,1,0:T(8,128)(2,1)S(1)}, u32[]{:S(2)}, u32[]{:S(2)}) collective-permute-start(bf16[4,128,256]{2,1,0:T(8,128)(2,1)S(1)} %get-tuple-element.56), channel_id=1, source_target_pairs={{6,0},{7,1},{0,2},{1,3},{2,4},{3,5},{4,6},{5,7},{14,8},{15,9},{8,1... | collective-permute-start | bytes 786440 | tf_op jit(solution)/shard_map/ppermute | solution.py:241
  104.0 4.5 %collective-permute-start.11 = (bf16[4,128,256]{2,1,0:T(8,128)(2,1)S(1)}, bf16[4,128,256]{2,1,0:T(8,128)(2,1)S(1)}, u32[]{:S(2)}, u32[]{:S(2)}) collective-permute-start(bf16[4,128,256]{2,1,0:T(8,128)(2,1)S(1)} %get-tuple-element.57), channel_id=1, source_target_pairs={{3,0},{2,1},{5,2},{4,3},{7,4},{6,5},{1,6},{0,7},{11,8},{10,9},{13,... | collective-permute-start | bytes 786440 | tf_op jit(solution)/shard_map/ppermute | solution.py:241
  108.5 0.0 collective-permute-done.7.refs_0_
  108.5 2.0 %collective-permute-start.12 = (bf16[4,128,256]{2,1,0:T(8,128)(2,1)S(1)}, bf16[4,128,256]{2,1,0:T(8,128)(2,1)S(1)}, u32[]{:S(2)}, u32[]{:S(2)}) collective-permute-start(bf16[4,128,256]{2,1,0:T(8,128)(2,1)S(1)} %get-tuple-element.58), channel_id=1, source_target_pairs={{7,0},{6,1},{1,2},{0,3},{3,4},{2,5},{5,6},{4,7},{15,8},{14,9},{9,1... | collective-permute-start | bytes 786440 | tf_op jit(solution)/shard_map/ppermute | solution.py:241
  110.5 0.0 collective-permute-done.8.refs_1_
  110.5 3.5 %collective-permute-start.13 = (bf16[4,128,256]{2,1,0:T(8,128)(2,1)S(1)}, bf16[4,128,256]{2,1,0:T(8,128)(2,1)S(1)}, u32[]{:S(2)}, u32[]{:S(2)}) collective-permute-start(bf16[4,128,256]{2,1,0:T(8,128)(2,1)S(1)} %get-tuple-element.59), channel_id=1, source_target_pairs={{1,0},{0,1},{3,2},{2,3},{5,4},{4,5},{7,6},{6,7},{9,8},{8,9},{11,10... | collective-permute-start | bytes 786440 | tf_op jit(solution)/shard_map/ppermute | solution.py:241
  114.0 0.0 collective-permute-done.9.refs_2_
  114.0 4.2 %collective-permute-done.10.refs_3_ = bf16[4,128,256]{2,1,0:T(8,128)(2,1)S(1)} collective-permute-done((bf16[4,128,256]{2,1,0:T(8,128)(2,1)S(1)}, bf16[4,128,256]{2,1,0:T(8,128)(2,1)S(1)}, u32[]{:S(2)}, u32[]{:S(2)}) %collective-permute-start.10) | collective-permute-done | bytes 262176 | tf_op jit(solution)/shard_map/ppermute | solution.py:241
  118.2 0.0 collective-permute-done.11.refs_4_
  118.2 11.6 %collective-permute-done.12.refs_5_ = bf16[4,128,256]{2,1,0:T(8,128)(2,1)S(1)} collective-permute-done((bf16[4,128,256]{2,1,0:T(8,128)(2,1)S(1)}, bf16[4,128,256]{2,1,0:T(8,128)(2,1)S(1)}, u32[]{:S(2)}, u32[]{:S(2)}) %collective-permute-start.12) | collective-permute-done | bytes 262176 | tf_op jit(solution)/shard_map/ppermute | solution.py:241
  129.8 0.0 collective-permute-done.13.refs_6_
  129.9 2.2 %unpack.1 = (bf16[128,2048]{1,0:T(8,128)(2,1)}, bf16[3,128,2048]{2,1,0:T(8,128)(2,1)}) custom-call(s32[2]{0:T(128)S(1)} %pad_add_fusion.place, bf16[4,128,256]{2,1,0:T(8,128)(2,1)S(1)} %collective-permute-done.7.refs_0_, bf16[4,128,256]{2,1,0:T(8,128)(2,1)S(1)} %collective-permute-done.8.refs_1_, bf16[4,128,256]{2,1,0:T(8,128)(2,1)S(1)} %collective-permute-done.9.refs_2_, ...), custom_call_target="tpu_custom_call" | custom-call | tf_op jit(solution)/shard_map/unpack/pallas_call | solution.py:223
  132.0 0.0 all-to-all-done.1
  132.0 0.7 copy.15
  (5 shorter events, 0.0 us)
Async XLA Ops:
  0.6 48.9 %copy-start = (bf16[256,256]{1,0:T(8,128)(2,1)S(1)}, bf16[256,256]{1,0:T(8,128)(2,1)}, u32[]{:S(2)}) copy-start(bf16[256,256]{1,0:T(8,128)(2,1)} %param.14) | copy-start | bytes 393220
  0.6 64.0 %copy-start.5 = (f32[128]{0:T(128)S(1)}, f32[128]{0:T(128)}, u32[]{:S(2)}) copy-start(f32[128]{0:T(128)} %param.17) | copy-start | bytes 1540
  0.7 64.0 %copy-start.4 = (f32[128]{0:T(128)S(1)}, f32[128]{0:T(128)}, u32[]{:S(2)}) copy-start(f32[128]{0:T(128)} %param.16) | copy-start | bytes 1540
  0.7 64.0 %copy-start.3 = (f32[128]{0:T(128)S(1)}, f32[128]{0:T(128)}, u32[]{:S(2)}) copy-start(f32[128]{0:T(128)} %param.15) | copy-start | bytes 1540
  0.8 1.4 %copy-start.1 = (bf16[1,128,3,2048]{3,1,2,0:T(8,128)(2,1)S(1)}, bf16[1,128,3,2048]{3,1,2,0:T(8,128)(2,1)}, u32[]{:S(2)}) copy-start(bf16[1,128,3,2048]{3,1,2,0:T(8,128)(2,1)} %param.9) | copy-start | bytes 4718596
  2.2 1.0 copy-start.2
  4.9 36.4 %collective-permute-start = (bf16[4,128,256]{2,1,0:T(8,128)(2,1)}, bf16[4,128,256]{2,1,0:T(8,128)(2,1)S(1)}, u32[]{:S(2)}, u32[]{:S(2)}) collective-permute-start(bf16[4,128,256]{2,1,0:T(8,128)(2,1)} %get-tuple-element.45), channel_id=1, source_target_pairs={{0,4},{1,5},{2,6},{3,7},{4,0},{5,1},{6,2},{7,3},{8,12},{9,13},{10,... | collective-permute-start | bytes 786440 | tf_op jit(solution)/shard_map/ppermute | solution.py:241
  15.8 31.0 %collective-permute-start.1 = (bf16[4,128,256]{2,1,0:T(8,128)(2,1)}, bf16[4,128,256]{2,1,0:T(8,128)(2,1)S(1)}, u32[]{:S(2)}, u32[]{:S(2)}) collective-permute-start(bf16[4,128,256]{2,1,0:T(8,128)(2,1)} %get-tuple-element.46), channel_id=1, source_target_pairs={{0,5},{1,4},{2,7},{3,6},{4,1},{5,0},{6,3},{7,2},{8,13},{9,12},{10,... | collective-permute-start | bytes 786440 | tf_op jit(solution)/shard_map/ppermute | solution.py:241
  17.7 32.0 %all-to-all-start = ((bf16[64,4,2,256]{3,2,1,0:T(2,128)(2,1)}), bf16[64,4,2,256]{3,2,1,0:T(2,128)(2,1)S(1)}, u32[]{:S(2)}, u32[]{:S(2)}) async-start(bf16[64,4,2,256]{3,2,1,0:T(2,128)(2,1)} %param.10), calls=%async_computation | async-start | bytes 524288 | tf_op jit(solution)/shard_map/all_to_all | solution.py:253
  29.4 29.8 %collective-permute-start.2 = (bf16[4,128,256]{2,1,0:T(8,128)(2,1)S(1)}, bf16[4,128,256]{2,1,0:T(8,128)(2,1)S(1)}, u32[]{:S(2)}, u32[]{:S(2)}) collective-permute-start(bf16[4,128,256]{2,1,0:T(8,128)(2,1)S(1)} %get-tuple-element.47), channel_id=1, source_target_pairs={{0,2},{1,3},{2,4},{3,5},{4,6},{5,7},{6,0},{7,1},{8,10},{9,11},{10,... | collective-permute-start | bytes 786440 | tf_op jit(solution)/shard_map/ppermute | solution.py:241
  33.7 25.5 %collective-permute-start.3 = (bf16[4,128,256]{2,1,0:T(8,128)(2,1)S(1)}, bf16[4,128,256]{2,1,0:T(8,128)(2,1)S(1)}, u32[]{:S(2)}, u32[]{:S(2)}) collective-permute-start(bf16[4,128,256]{2,1,0:T(8,128)(2,1)S(1)} %get-tuple-element.48), channel_id=1, source_target_pairs={{0,6},{1,7},{2,0},{3,1},{4,2},{5,3},{6,4},{7,5},{8,14},{9,15},{10,... | collective-permute-start | bytes 786440 | tf_op jit(solution)/shard_map/ppermute | solution.py:241
  38.4 26.3 %collective-permute-start.4 = (bf16[4,128,256]{2,1,0:T(8,128)(2,1)S(1)}, bf16[4,128,256]{2,1,0:T(8,128)(2,1)S(1)}, u32[]{:S(2)}, u32[]{:S(2)}) collective-permute-start(bf16[4,128,256]{2,1,0:T(8,128)(2,1)S(1)} %get-tuple-element.49), channel_id=1, source_target_pairs={{0,3},{1,2},{2,5},{3,4},{4,7},{5,6},{6,1},{7,0},{8,11},{9,10},{10,... | collective-permute-start | bytes 786440 | tf_op jit(solution)/shard_map/ppermute | solution.py:241
  41.2 23.4 %collective-permute-start.5 = (bf16[4,128,256]{2,1,0:T(8,128)(2,1)S(1)}, bf16[4,128,256]{2,1,0:T(8,128)(2,1)}, u32[]{:S(2)}, u32[]{:S(2)}) collective-permute-start(bf16[4,128,256]{2,1,0:T(8,128)(2,1)S(1)} %get-tuple-element.50), channel_id=1, source_target_pairs={{0,7},{1,6},{2,1},{3,0},{4,3},{5,2},{6,5},{7,4},{8,15},{9,14},{10,... | collective-permute-start | bytes 786440 | tf_op jit(solution)/shard_map/ppermute | solution.py:241
  46.7 17.9 %collective-permute-start.6 = (bf16[4,128,256]{2,1,0:T(8,128)(2,1)S(1)}, bf16[4,128,256]{2,1,0:T(8,128)(2,1)}, u32[]{:S(2)}, u32[]{:S(2)}) collective-permute-start(bf16[4,128,256]{2,1,0:T(8,128)(2,1)S(1)} %get-tuple-element.51), channel_id=1, source_target_pairs={{0,1},{1,0},{2,3},{3,2},{4,5},{5,4},{6,7},{7,6},{8,9},{9,8},{10,11... | collective-permute-start | bytes 786440 | tf_op jit(solution)/shard_map/ppermute | solution.py:241
  74.7 33.8 %collective-permute-start.7 = (bf16[4,128,256]{2,1,0:T(8,128)(2,1)}, bf16[4,128,256]{2,1,0:T(8,128)(2,1)S(1)}, u32[]{:S(2)}, u32[]{:S(2)}) collective-permute-start(bf16[4,128,256]{2,1,0:T(8,128)(2,1)} %get-tuple-element.53), channel_id=1, source_target_pairs={{4,0},{5,1},{6,2},{7,3},{0,4},{1,5},{2,6},{3,7},{12,8},{13,9},{14,... | collective-permute-start | bytes 786440 | tf_op jit(solution)/shard_map/ppermute | solution.py:241
  81.8 28.6 %collective-permute-start.8 = (bf16[4,128,256]{2,1,0:T(8,128)(2,1)}, bf16[4,128,256]{2,1,0:T(8,128)(2,1)S(1)}, u32[]{:S(2)}, u32[]{:S(2)}) collective-permute-start(bf16[4,128,256]{2,1,0:T(8,128)(2,1)} %get-tuple-element.54), channel_id=1, source_target_pairs={{5,0},{4,1},{7,2},{6,3},{1,4},{0,5},{3,6},{2,7},{13,8},{12,9},{15,... | collective-permute-start | bytes 786440 | tf_op jit(solution)/shard_map/ppermute | solution.py:241
  85.0 47.0 %all-to-all-start.1 = ((bf16[64,4,2,256]{3,2,1,0:T(2,128)(2,1)}), bf16[64,4,2,256]{3,2,1,0:T(2,128)(2,1)S(1)}, u32[]{:S(2)}, u32[]{:S(2)}) async-start(bf16[64,4,2,256]{3,2,1,0:T(2,128)(2,1)} %bitcast.16), calls=%async_computation.1 | async-start | bytes 524288 | tf_op jit(solution)/shard_map/all_to_all | solution.py:267
  96.9 17.1 %collective-permute-start.9 = (bf16[4,128,256]{2,1,0:T(8,128)(2,1)S(1)}, bf16[4,128,256]{2,1,0:T(8,128)(2,1)S(1)}, u32[]{:S(2)}, u32[]{:S(2)}) collective-permute-start(bf16[4,128,256]{2,1,0:T(8,128)(2,1)S(1)} %get-tuple-element.55), channel_id=1, source_target_pairs={{2,0},{3,1},{4,2},{5,3},{6,4},{7,5},{0,6},{1,7},{10,8},{11,9},{12,... | collective-permute-start | bytes 786440 | tf_op jit(solution)/shard_map/ppermute | solution.py:241
  102.0 16.2 %collective-permute-start.10 = (bf16[4,128,256]{2,1,0:T(8,128)(2,1)S(1)}, bf16[4,128,256]{2,1,0:T(8,128)(2,1)S(1)}, u32[]{:S(2)}, u32[]{:S(2)}) collective-permute-start(bf16[4,128,256]{2,1,0:T(8,128)(2,1)S(1)} %get-tuple-element.56), channel_id=1, source_target_pairs={{6,0},{7,1},{0,2},{1,3},{2,4},{3,5},{4,6},{5,7},{14,8},{15,9},{8,1... | collective-permute-start | bytes 786440 | tf_op jit(solution)/shard_map/ppermute | solution.py:241
  104.0 14.2 %collective-permute-start.11 = (bf16[4,128,256]{2,1,0:T(8,128)(2,1)S(1)}, bf16[4,128,256]{2,1,0:T(8,128)(2,1)S(1)}, u32[]{:S(2)}, u32[]{:S(2)}) collective-permute-start(bf16[4,128,256]{2,1,0:T(8,128)(2,1)S(1)} %get-tuple-element.57), channel_id=1, source_target_pairs={{3,0},{2,1},{5,2},{4,3},{7,4},{6,5},{1,6},{0,7},{11,8},{10,9},{13,... | collective-permute-start | bytes 786440 | tf_op jit(solution)/shard_map/ppermute | solution.py:241
  108.5 21.4 %collective-permute-start.12 = (bf16[4,128,256]{2,1,0:T(8,128)(2,1)S(1)}, bf16[4,128,256]{2,1,0:T(8,128)(2,1)S(1)}, u32[]{:S(2)}, u32[]{:S(2)}) collective-permute-start(bf16[4,128,256]{2,1,0:T(8,128)(2,1)S(1)} %get-tuple-element.58), channel_id=1, source_target_pairs={{7,0},{6,1},{1,2},{0,3},{3,4},{2,5},{5,6},{4,7},{15,8},{14,9},{9,1... | collective-permute-start | bytes 786440 | tf_op jit(solution)/shard_map/ppermute | solution.py:241
  110.5 19.4 %collective-permute-start.13 = (bf16[4,128,256]{2,1,0:T(8,128)(2,1)S(1)}, bf16[4,128,256]{2,1,0:T(8,128)(2,1)S(1)}, u32[]{:S(2)}, u32[]{:S(2)}) collective-permute-start(bf16[4,128,256]{2,1,0:T(8,128)(2,1)S(1)} %get-tuple-element.59), channel_id=1, source_target_pairs={{1,0},{0,1},{3,2},{2,3},{5,4},{4,5},{7,6},{6,7},{9,8},{8,9},{11,10... | collective-permute-start | bytes 786440 | tf_op jit(solution)/shard_map/ppermute | solution.py:241

commit v4 on v3

--- a/solution.py
+++ b/solution.py
@@ -73,15 +73,18 @@
             out[3] = cot[:, columns]
 
 
-def unpack_kernel(place, *refs):
-    packed, (out, grads) = refs[:-2], refs[-2:]
-    for h in range(OUT_PARTS):
-        for k, offset in enumerate(OFFSETS):
-            part = packed[h * SEQ + k]
-            d = partner(place[0], place[1], offset)
-            columns = pl.ds(pl.multiple_of(d * WIDTH + h * OUT_WIDTH, OUT_WIDTH), OUT_WIDTH)
-            out[:, columns] = part[0]
-            grads[:, :, columns] = part[1:]
+def unpack_kernel(place, d_txt, *refs):
+    packed, (out, grads, prompt_out, sems) = refs[:SEQ], refs[SEQ:]
+    copies = [pltpu.make_async_copy(d_txt, prompt_out, sems.at[SEQ, 0])]
+    for k, offset in enumerate(OFFSETS):
+        d = partner(place[0], place[1], offset)
+        columns = pl.ds(pl.multiple_of(d * WIDTH, WIDTH), WIDTH)
+        copies.append(pltpu.make_async_copy(packed[k].at[0], out.at[:, columns], sems.at[k, 0]))
+        copies.append(pltpu.make_async_copy(packed[k].at[pl.ds(1, 3)], grads.at[:, :, columns], sems.at[k, 1]))
+    for copy in copies:
+        copy.start()
+    for copy in copies:
+        copy.wait()
 
 
 def split_kernel(txt, tk, tv):
@@ -219,18 +222,20 @@
     )(dtk, dtv)
 
 
-def unpack(place, packed):
+def unpack(place, d_txt, packed):
     return pl.pallas_call(
         unpack_kernel,
         out_shape=(
             jax.ShapeDtypeStruct((ROWS, D), jnp.bfloat16),
             jax.ShapeDtypeStruct((3, ROWS, D), jnp.bfloat16),
+            jax.ShapeDtypeStruct(d_txt.shape, jnp.bfloat16),
         ),
-        in_specs=[SMEM] + [VMEM] * (SEQ * OUT_PARTS),
-        out_specs=(VMEM, VMEM),
+        in_specs=[SMEM] + [ANY] * (1 + SEQ),
+        out_specs=(ANY, ANY, ANY),
+        scratch_shapes=[pltpu.SemaphoreType.DMA((SEQ + 1, 2))],
         compiler_params=pltpu.CompilerParams(vmem_limit_bytes=16 * 1024 * 1024),
         name="unpack",
-    )(place, *packed)
+    )(place, d_txt, *packed)
 
 
 def exchange(parts, way):
@@ -265,7 +270,7 @@
         d_prompt.append(merge(dtk, dtv))
     d_txt = jnp.concatenate(d_prompt, axis=-1).reshape(samples, text_rows, 2, WIDTH)
     d_txt = lax.all_to_all(d_txt, groups, split_axis=0, concat_axis=0, tiled=True)
-    out, grads = unpack(place, returned)
+    out, grads, d_txt = unpack(place, d_txt, returned)
     return out[None], grads.transpose(1, 0, 2)[None], d_txt
 
 

time: 134 us -> 133 us (level)
    unnamed x13 -> x12, local copies, waits for them, and re-layouts: 3.17 us -> 2.47 us
  transfers between devices with their start and end apart: 16 -> 16, of which waited for: 4 -> 5; matrix products, arithmetic and copies ran while one was open for 0% -> 0% of each run, Pallas kernels for 3% -> 1%
where the time goes in v4:
time: 133 us; the launch traced here: 132 us
  starting transfers between devices  81.3 us (61%)
  waiting for transfers between devices  30.3 us (23%)
  Pallas kernels  15.7 us (12%)
  local copies, waits for them, and re-layouts  2.47 us (2%)
  between operations  2.2 us (2%)
    ppermute x14, starting transfers between devices, exchange(): lax.ppermute(part, 'seq', pairs if way == 1 else [(b, a) for a, b in pairs])  57.8 us
    ppermute x14, waiting for transfers between devices, exchange(): lax.ppermute(part, 'seq', pairs if way == 1 else [(b, a) for a, b in pairs])  30.3 us
    all_to_all x1, starting transfers between devices, local(): lax.all_to_all(d_txt, groups, split_axis=0, concat_axis=0, tiled=True)  11.8 us
    all_to_all x1, starting transfers between devices, local(): lax.all_to_all(txt_kv, groups, split_axis=0, concat_axis=0, tiled=True)  11.7 us
    pallas_call x1, Pallas kernels, attend(): pl.pallas_call(functools.partial(attend_kernel, first, count), out_shape=...  10.2 us
  transfers between devices with their start and end apart: 16, of which 5 were waited for; matrix products, arithmetic and copies ran while one was open for 0% of the time, Pallas kernels for 1%

profile of v4, /device:TPU:6, one launch (start us, length us, event | category | flops | bytes accessed | tf_op | source)
XLA Modules:
  0.0 132.2 jit_solution(11470149341716120503)
XLA Ops:
  0.6 0.0 copy-start
  0.6 0.0 copy-start.5
  0.7 0.0 copy-start.4
  0.7 0.0 copy-start.3
  0.7 0.1 pad_add_fusion.place
  0.8 1.4 %copy-done.1 = bf16[1,128,3,2048]{3,1,2,0:T(8,128)(2,1)S(1)} copy-done((bf16[1,128,3,2048]{3,1,2,0:T(8,128)(2,1)S(1)}, bf16[1,128,3,2048]{3,1,2,0:T(8,128)(2,1)}, u32[]{:S(2)}) %copy-start.1) | copy-done | bytes 1572888
  2.2 1.0 copy-done.2
  3.2 1.6 %pack.1 = (bf16[4,128,256]{2,1,0:T(8,128)(2,1)}, bf16[4,128,256]{2,1,0:T(8,128)(2,1)}, bf16[4,128,256]{2,1,0:T(8,128)(2,1)S(1)}, bf16[4,128,256]{2,1,0:T(8,128)(...) custom-call(s32[2]{0:T(128)S(1)} %pad_add_fusion.place, ...), custom_call_target="tpu_custom_call" | custom-call | tf_op jit(solution)/shard_map/pack/pallas_call | solution.py:193
  4.9 10.9 %collective-permute-start = (bf16[4,128,256]{2,1,0:T(8,128)(2,1)}, bf16[4,128,256]{2,1,0:T(8,128)(2,1)S(1)}, u32[]{:S(2)}, u32[]{:S(2)}) collective-permute-start(bf16[4,128,256]{2,1,0:T(8,128)(2,1)} %get-tuple-element.46), channel_id=1, source_target_pairs={{0,4},{1,5},{2,6},{3,7},{4,0},{5,1},{6,2},{7,3},{8,12},{9,13},{10,... | collective-permute-start | bytes 786440 | tf_op jit(solution)/shard_map/ppermute | solution.py:246
  15.8 1.9 %collective-permute-start.1 = (bf16[4,128,256]{2,1,0:T(8,128)(2,1)}, bf16[4,128,256]{2,1,0:T(8,128)(2,1)S(1)}, u32[]{:S(2)}, u32[]{:S(2)}) collective-permute-start(bf16[4,128,256]{2,1,0:T(8,128)(2,1)} %get-tuple-element.47), channel_id=1, source_target_pairs={{0,5},{1,4},{2,7},{3,6},{4,1},{5,0},{6,3},{7,2},{8,13},{9,12},{10,... | collective-permute-start | bytes 786440 | tf_op jit(solution)/shard_map/ppermute | solution.py:246
  17.7 11.7 %all-to-all-start = ((bf16[64,4,2,256]{3,2,1,0:T(2,128)(2,1)}), bf16[64,4,2,256]{3,2,1,0:T(2,128)(2,1)S(1)}, u32[]{:S(2)}, u32[]{:S(2)}) async-start(bf16[64,4,2,256]{3,2,1,0:T(2,128)(2,1)} %param.10), calls=%async_computation | async-start | bytes 524288 | tf_op jit(solution)/shard_map/all_to_all | solution.py:258
  29.4 4.3 %collective-permute-start.2 = (bf16[4,128,256]{2,1,0:T(8,128)(2,1)S(1)}, bf16[4,128,256]{2,1,0:T(8,128)(2,1)S(1)}, u32[]{:S(2)}, u32[]{:S(2)}) collective-permute-start(bf16[4,128,256]{2,1,0:T(8,128)(2,1)S(1)} %get-tuple-element.48), channel_id=1, source_target_pairs={{0,2},{1,3},{2,4},{3,5},{4,6},{5,7},{6,0},{7,1},{8,10},{9,11},{10,... | collective-permute-start | bytes 786440 | tf_op jit(solution)/shard_map/ppermute | solution.py:246
  33.7 4.6 %collective-permute-start.3 = (bf16[4,128,256]{2,1,0:T(8,128)(2,1)S(1)}, bf16[4,128,256]{2,1,0:T(8,128)(2,1)S(1)}, u32[]{:S(2)}, u32[]{:S(2)}) collective-permute-start(bf16[4,128,256]{2,1,0:T(8,128)(2,1)S(1)} %get-tuple-element.49), channel_id=1, source_target_pairs={{0,6},{1,7},{2,0},{3,1},{4,2},{5,3},{6,4},{7,5},{8,14},{9,15},{10,... | collective-permute-start | bytes 786440 | tf_op jit(solution)/shard_map/ppermute | solution.py:246
  38.4 2.2 %collective-permute-start.4 = (bf16[4,128,256]{2,1,0:T(8,128)(2,1)S(1)}, bf16[4,128,256]{2,1,0:T(8,128)(2,1)S(1)}, u32[]{:S(2)}, u32[]{:S(2)}) collective-permute-start(bf16[4,128,256]{2,1,0:T(8,128)(2,1)S(1)} %get-tuple-element.50), channel_id=1, source_target_pairs={{0,3},{1,2},{2,5},{3,4},{4,7},{5,6},{6,1},{7,0},{8,11},{9,10},{10,... | collective-permute-start | bytes 786440 | tf_op jit(solution)/shard_map/ppermute | solution.py:246
  41.2 0.0 collective-permute-done.refs_0_
  41.2 5.5 %collective-permute-start.5 = (bf16[4,128,256]{2,1,0:T(8,128)(2,1)S(1)}, bf16[4,128,256]{2,1,0:T(8,128)(2,1)}, u32[]{:S(2)}, u32[]{:S(2)}) collective-permute-start(bf16[4,128,256]{2,1,0:T(8,128)(2,1)S(1)} %get-tuple-element.51), channel_id=1, source_target_pairs={{0,7},{1,6},{2,1},{3,0},{4,3},{5,2},{6,5},{7,4},{8,15},{9,14},{10,... | collective-permute-start | bytes 786440 | tf_op jit(solution)/shard_map/ppermute | solution.py:246
  46.7 0.0 collective-permute-done.1.refs_1_
  46.7 2.1 %collective-permute-start.6 = (bf16[4,128,256]{2,1,0:T(8,128)(2,1)S(1)}, bf16[4,128,256]{2,1,0:T(8,128)(2,1)}, u32[]{:S(2)}, u32[]{:S(2)}) collective-permute-start(bf16[4,128,256]{2,1,0:T(8,128)(2,1)S(1)} %get-tuple-element.52), channel_id=1, source_target_pairs={{0,1},{1,0},{2,3},{3,2},{4,5},{5,4},{6,7},{7,6},{8,9},{9,8},{10,11... | collective-permute-start | bytes 786440 | tf_op jit(solution)/shard_map/ppermute | solution.py:246
  48.8 0.1 fusion.3
  49.5 0.1 fusion.gate
  49.7 0.0 all-to-all-done
  49.7 0.6 split.1
  50.3 8.9 %collective-permute-done.2.refs_2_ = bf16[4,128,256]{2,1,0:T(8,128)(2,1)S(1)} collective-permute-done((bf16[4,128,256]{2,1,0:T(8,128)(2,1)S(1)}, bf16[4,128,256]{2,1,0:T(8,128)(2,1)S(1)}, u32[]{:S(2)}, u32[]{:S(2)}) %collective-permute-start.2) | collective-permute-done | bytes 262176 | tf_op jit(solution)/shard_map/ppermute | solution.py:246
  59.2 0.0 collective-permute-done.3.refs_3_
  59.2 5.5 %collective-permute-done.4.refs_4_ = bf16[4,128,256]{2,1,0:T(8,128)(2,1)S(1)} collective-permute-done((bf16[4,128,256]{2,1,0:T(8,128)(2,1)S(1)}, bf16[4,128,256]{2,1,0:T(8,128)(2,1)S(1)}, u32[]{:S(2)}, u32[]{:S(2)}) %collective-permute-start.4) | collective-permute-done | bytes 262176 | tf_op jit(solution)/shard_map/ppermute | solution.py:246
  64.7 0.0 collective-permute-done.5.refs_5_
  64.7 0.0 collective-permute-done.6.refs_6_
  64.7 0.0 copy-done.4
  64.7 0.0 copy-done.3
  64.7 10.2 %attend.1 = (bf16[4,128,256]{2,1,0:T(8,128)(2,1)}, bf16[4,128,256]{2,1,0:T(8,128)(2,1)}, bf16[4,128,256]{2,1,0:T(8,128)(2,1)}, bf16[4,128,256]{2,1,0:T(8,128)(2,...) custom-call(s32[1]{0:T(128)S(6)} %copy.13.length, ...), custom_call_target="tpu_custom_call" | custom-call | flops 4026531840 | bytes 8388608 | tf_op jit(solution)/shard_map/attend/pallas_call | solution.py:178
  74.9 7.2 %collective-permute-start.7 = (bf16[4,128,256]{2,1,0:T(8,128)(2,1)}, bf16[4,128,256]{2,1,0:T(8,128)(2,1)S(1)}, u32[]{:S(2)}, u32[]{:S(2)}) collective-permute-start(bf16[4,128,256]{2,1,0:T(8,128)(2,1)} %get-tuple-element.56), channel_id=1, source_target_pairs={{4,0},{5,1},{6,2},{7,3},{0,4},{1,5},{2,6},{3,7},{12,8},{13,9},{14,... | collective-permute-start | bytes 786440 | tf_op jit(solution)/shard_map/ppermute | solution.py:246
  82.1 2.0 %collective-permute-start.8 = (bf16[4,128,256]{2,1,0:T(8,128)(2,1)}, bf16[4,128,256]{2,1,0:T(8,128)(2,1)S(1)}, u32[]{:S(2)}, u32[]{:S(2)}) collective-permute-start(bf16[4,128,256]{2,1,0:T(8,128)(2,1)} %get-tuple-element.57), channel_id=1, source_target_pairs={{5,0},{4,1},{7,2},{6,3},{1,4},{0,5},{3,6},{2,7},{13,8},{12,9},{15,... | collective-permute-start | bytes 786440 | tf_op jit(solution)/shard_map/ppermute | solution.py:246
  84.1 1.2 merge.1
  85.2 11.8 %all-to-all-start.1 = ((bf16[64,4,2,256]{3,2,1,0:T(2,128)(2,1)}), bf16[64,4,2,256]{3,2,1,0:T(2,128)(2,1)S(1)}, u32[]{:S(2)}, u32[]{:S(2)}) async-start(bf16[64,4,2,256]{3,2,1,0:T(2,128)(2,1)} %bitcast.13), calls=%async_computation.1 | async-start | bytes 524288 | tf_op jit(solution)/shard_map/all_to_all | solution.py:272
  97.0 5.2 %collective-permute-start.9 = (bf16[4,128,256]{2,1,0:T(8,128)(2,1)}, bf16[4,128,256]{2,1,0:T(8,128)(2,1)S(1)}, u32[]{:S(2)}, u32[]{:S(2)}) collective-permute-start(bf16[4,128,256]{2,1,0:T(8,128)(2,1)} %get-tuple-element.58), channel_id=1, source_target_pairs={{2,0},{3,1},{4,2},{5,3},{6,4},{7,5},{0,6},{1,7},{10,8},{11,9},{12,... | collective-permute-start | bytes 786440 | tf_op jit(solution)/shard_map/ppermute | solution.py:246
  102.3 1.9 %collective-permute-start.10 = (bf16[4,128,256]{2,1,0:T(8,128)(2,1)}, bf16[4,128,256]{2,1,0:T(8,128)(2,1)S(1)}, u32[]{:S(2)}, u32[]{:S(2)}) collective-permute-start(bf16[4,128,256]{2,1,0:T(8,128)(2,1)} %get-tuple-element.59), channel_id=1, source_target_pairs={{6,0},{7,1},{0,2},{1,3},{2,4},{3,5},{4,6},{5,7},{14,8},{15,9},{8,1... | collective-permute-start | bytes 786440 | tf_op jit(solution)/shard_map/ppermute | solution.py:246
  104.2 4.5 %collective-permute-start.11 = (bf16[4,128,256]{2,1,0:T(8,128)(2,1)S(1)}, bf16[4,128,256]{2,1,0:T(8,128)(2,1)S(1)}, u32[]{:S(2)}, u32[]{:S(2)}) collective-permute-start(bf16[4,128,256]{2,1,0:T(8,128)(2,1)S(1)} %get-tuple-element.60), channel_id=1, source_target_pairs={{3,0},{2,1},{5,2},{4,3},{7,4},{6,5},{1,6},{0,7},{11,8},{10,9},{13,... | collective-permute-start | bytes 786440 | tf_op jit(solution)/shard_map/ppermute | solution.py:246
  108.7 0.0 collective-permute-done.7.refs_0_
  108.7 2.0 %collective-permute-start.12 = (bf16[4,128,256]{2,1,0:T(8,128)(2,1)S(1)}, bf16[4,128,256]{2,1,0:T(8,128)(2,1)S(1)}, u32[]{:S(2)}, u32[]{:S(2)}) collective-permute-start(bf16[4,128,256]{2,1,0:T(8,128)(2,1)S(1)} %get-tuple-element.61), channel_id=1, source_target_pairs={{7,0},{6,1},{1,2},{0,3},{3,4},{2,5},{5,6},{4,7},{15,8},{14,9},{9,1... | collective-permute-start | bytes 786440 | tf_op jit(solution)/shard_map/ppermute | solution.py:246
  110.7 0.0 collective-permute-done.8.refs_1_
  110.7 3.5 %collective-permute-start.13 = (bf16[4,128,256]{2,1,0:T(8,128)(2,1)S(1)}, bf16[4,128,256]{2,1,0:T(8,128)(2,1)S(1)}, u32[]{:S(2)}, u32[]{:S(2)}) collective-permute-start(bf16[4,128,256]{2,1,0:T(8,128)(2,1)S(1)} %get-tuple-element.62), channel_id=1, source_target_pairs={{1,0},{0,1},{3,2},{2,3},{5,4},{4,5},{7,6},{6,7},{9,8},{8,9},{11,10... | collective-permute-start | bytes 786440 | tf_op jit(solution)/shard_map/ppermute | solution.py:246
  114.2 0.0 collective-permute-done.9.refs_2_
  114.2 3.4 %collective-permute-done.10.refs_3_ = bf16[4,128,256]{2,1,0:T(8,128)(2,1)S(1)} collective-permute-done((bf16[4,128,256]{2,1,0:T(8,128)(2,1)}, bf16[4,128,256]{2,1,0:T(8,128)(2,1)S(1)}, u32[]{:S(2)}, u32[]{:S(2)}) %collective-permute-start.10) | collective-permute-done | bytes 262176 | tf_op jit(solution)/shard_map/ppermute | solution.py:246
  117.6 0.8 collective-permute-done.11.refs_4_
  118.4 11.7 %collective-permute-done.12.refs_5_ = bf16[4,128,256]{2,1,0:T(8,128)(2,1)S(1)} collective-permute-done((bf16[4,128,256]{2,1,0:T(8,128)(2,1)S(1)}, bf16[4,128,256]{2,1,0:T(8,128)(2,1)S(1)}, u32[]{:S(2)}, u32[]{:S(2)}) %collective-permute-start.12) | collective-permute-done | bytes 262176 | tf_op jit(solution)/shard_map/ppermute | solution.py:246
  130.1 0.0 collective-permute-done.13.refs_6_
  130.1 0.0 all-to-all-done.1.d_txt
  130.1 2.1 %unpack.1 = (bf16[128,2048]{1,0:T(8,128)(2,1)}, bf16[3,128,2048]{2,1,0:T(8,128)(2,1)}, bf16[64,4,2,256]{3,2,1,0:T(2,128)(2,1)}) custom-call(s32[2]{0:T(128)S(1)} %pad_add_fusion.place, bf16[64,4,2,256]{3,2,1,0:T(2,128)(2,1)S(1)} %all-to-all-done.1.d_txt, bf16[4,128,256]{2,1,0:T(8,128)(2,1)S(1)} %collective-permute-done.7.refs_0_, ...), custom_call_target="tpu_custom_call" | custom-call | tf_op jit(solution)/shard_map/unpack/pallas_call | solution.py:226
  (4 shorter events, 0.0 us)
Async XLA Ops:
  0.6 48.9 %copy-start = (bf16[256,256]{1,0:T(8,128)(2,1)S(1)}, bf16[256,256]{1,0:T(8,128)(2,1)}, u32[]{:S(2)}) copy-start(bf16[256,256]{1,0:T(8,128)(2,1)} %param.14) | copy-start | bytes 393220
  0.6 64.0 %copy-start.5 = (f32[128]{0:T(128)S(1)}, f32[128]{0:T(128)}, u32[]{:S(2)}) copy-start(f32[128]{0:T(128)} %param.17) | copy-start | bytes 1540
  0.7 64.0 %copy-start.4 = (f32[128]{0:T(128)S(1)}, f32[128]{0:T(128)}, u32[]{:S(2)}) copy-start(f32[128]{0:T(128)} %param.16) | copy-start | bytes 1540
  0.7 64.0 %copy-start.3 = (f32[128]{0:T(128)S(1)}, f32[128]{0:T(128)}, u32[]{:S(2)}) copy-start(f32[128]{0:T(128)} %param.15) | copy-start | bytes 1540
  0.8 1.4 %copy-start.1 = (bf16[1,128,3,2048]{3,1,2,0:T(8,128)(2,1)S(1)}, bf16[1,128,3,2048]{3,1,2,0:T(8,128)(2,1)}, u32[]{:S(2)}) copy-start(bf16[1,128,3,2048]{3,1,2,0:T(8,128)(2,1)} %param.9) | copy-start | bytes 4718596
  2.2 1.0 copy-start.2
  4.9 36.4 %collective-permute-start = (bf16[4,128,256]{2,1,0:T(8,128)(2,1)}, bf16[4,128,256]{2,1,0:T(8,128)(2,1)S(1)}, u32[]{:S(2)}, u32[]{:S(2)}) collective-permute-start(bf16[4,128,256]{2,1,0:T(8,128)(2,1)} %get-tuple-element.46), channel_id=1, source_target_pairs={{0,4},{1,5},{2,6},{3,7},{4,0},{5,1},{6,2},{7,3},{8,12},{9,13},{10,... | collective-permute-start | bytes 786440 | tf_op jit(solution)/shard_map/ppermute | solution.py:246
  15.8 31.0 %collective-permute-start.1 = (bf16[4,128,256]{2,1,0:T(8,128)(2,1)}, bf16[4,128,256]{2,1,0:T(8,128)(2,1)S(1)}, u32[]{:S(2)}, u32[]{:S(2)}) collective-permute-start(bf16[4,128,256]{2,1,0:T(8,128)(2,1)} %get-tuple-element.47), channel_id=1, source_target_pairs={{0,5},{1,4},{2,7},{3,6},{4,1},{5,0},{6,3},{7,2},{8,13},{9,12},{10,... | collective-permute-start | bytes 786440 | tf_op jit(solution)/shard_map/ppermute | solution.py:246
  17.7 32.0 %all-to-all-start = ((bf16[64,4,2,256]{3,2,1,0:T(2,128)(2,1)}), bf16[64,4,2,256]{3,2,1,0:T(2,128)(2,1)S(1)}, u32[]{:S(2)}, u32[]{:S(2)}) async-start(bf16[64,4,2,256]{3,2,1,0:T(2,128)(2,1)} %param.10), calls=%async_computation | async-start | bytes 524288 | tf_op jit(solution)/shard_map/all_to_all | solution.py:258
  29.4 29.8 %collective-permute-start.2 = (bf16[4,128,256]{2,1,0:T(8,128)(2,1)S(1)}, bf16[4,128,256]{2,1,0:T(8,128)(2,1)S(1)}, u32[]{:S(2)}, u32[]{:S(2)}) collective-permute-start(bf16[4,128,256]{2,1,0:T(8,128)(2,1)S(1)} %get-tuple-element.48), channel_id=1, source_target_pairs={{0,2},{1,3},{2,4},{3,5},{4,6},{5,7},{6,0},{7,1},{8,10},{9,11},{10,... | collective-permute-start | bytes 786440 | tf_op jit(solution)/shard_map/ppermute | solution.py:246
  33.7 25.5 %collective-permute-start.3 = (bf16[4,128,256]{2,1,0:T(8,128)(2,1)S(1)}, bf16[4,128,256]{2,1,0:T(8,128)(2,1)S(1)}, u32[]{:S(2)}, u32[]{:S(2)}) collective-permute-start(bf16[4,128,256]{2,1,0:T(8,128)(2,1)S(1)} %get-tuple-element.49), channel_id=1, source_target_pairs={{0,6},{1,7},{2,0},{3,1},{4,2},{5,3},{6,4},{7,5},{8,14},{9,15},{10,... | collective-permute-start | bytes 786440 | tf_op jit(solution)/shard_map/ppermute | solution.py:246
  38.4 26.3 %collective-permute-start.4 = (bf16[4,128,256]{2,1,0:T(8,128)(2,1)S(1)}, bf16[4,128,256]{2,1,0:T(8,128)(2,1)S(1)}, u32[]{:S(2)}, u32[]{:S(2)}) collective-permute-start(bf16[4,128,256]{2,1,0:T(8,128)(2,1)S(1)} %get-tuple-element.50), channel_id=1, source_target_pairs={{0,3},{1,2},{2,5},{3,4},{4,7},{5,6},{6,1},{7,0},{8,11},{9,10},{10,... | collective-permute-start | bytes 786440 | tf_op jit(solution)/shard_map/ppermute | solution.py:246
  41.2 23.4 %collective-permute-start.5 = (bf16[4,128,256]{2,1,0:T(8,128)(2,1)S(1)}, bf16[4,128,256]{2,1,0:T(8,128)(2,1)}, u32[]{:S(2)}, u32[]{:S(2)}) collective-permute-start(bf16[4,128,256]{2,1,0:T(8,128)(2,1)S(1)} %get-tuple-element.51), channel_id=1, source_target_pairs={{0,7},{1,6},{2,1},{3,0},{4,3},{5,2},{6,5},{7,4},{8,15},{9,14},{10,... | collective-permute-start | bytes 786440 | tf_op jit(solution)/shard_map/ppermute | solution.py:246
  46.7 17.9 %collective-permute-start.6 = (bf16[4,128,256]{2,1,0:T(8,128)(2,1)S(1)}, bf16[4,128,256]{2,1,0:T(8,128)(2,1)}, u32[]{:S(2)}, u32[]{:S(2)}) collective-permute-start(bf16[4,128,256]{2,1,0:T(8,128)(2,1)S(1)} %get-tuple-element.52), channel_id=1, source_target_pairs={{0,1},{1,0},{2,3},{3,2},{4,5},{5,4},{6,7},{7,6},{8,9},{9,8},{10,11... | collective-permute-start | bytes 786440 | tf_op jit(solution)/shard_map/ppermute | solution.py:246
  74.9 33.8 %collective-permute-start.7 = (bf16[4,128,256]{2,1,0:T(8,128)(2,1)}, bf16[4,128,256]{2,1,0:T(8,128)(2,1)S(1)}, u32[]{:S(2)}, u32[]{:S(2)}) collective-permute-start(bf16[4,128,256]{2,1,0:T(8,128)(2,1)} %get-tuple-element.56), channel_id=1, source_target_pairs={{4,0},{5,1},{6,2},{7,3},{0,4},{1,5},{2,6},{3,7},{12,8},{13,9},{14,... | collective-permute-start | bytes 786440 | tf_op jit(solution)/shard_map/ppermute | solution.py:246
  82.1 28.6 %collective-permute-start.8 = (bf16[4,128,256]{2,1,0:T(8,128)(2,1)}, bf16[4,128,256]{2,1,0:T(8,128)(2,1)S(1)}, u32[]{:S(2)}, u32[]{:S(2)}) collective-permute-start(bf16[4,128,256]{2,1,0:T(8,128)(2,1)} %get-tuple-element.57), channel_id=1, source_target_pairs={{5,0},{4,1},{7,2},{6,3},{1,4},{0,5},{3,6},{2,7},{13,8},{12,9},{15,... | collective-permute-start | bytes 786440 | tf_op jit(solution)/shard_map/ppermute | solution.py:246
  85.2 44.8 %all-to-all-start.1 = ((bf16[64,4,2,256]{3,2,1,0:T(2,128)(2,1)}), bf16[64,4,2,256]{3,2,1,0:T(2,128)(2,1)S(1)}, u32[]{:S(2)}, u32[]{:S(2)}) async-start(bf16[64,4,2,256]{3,2,1,0:T(2,128)(2,1)} %bitcast.13), calls=%async_computation.1 | async-start | bytes 524288 | tf_op jit(solution)/shard_map/all_to_all | solution.py:272
  97.0 17.2 %collective-permute-start.9 = (bf16[4,128,256]{2,1,0:T(8,128)(2,1)}, bf16[4,128,256]{2,1,0:T(8,128)(2,1)S(1)}, u32[]{:S(2)}, u32[]{:S(2)}) collective-permute-start(bf16[4,128,256]{2,1,0:T(8,128)(2,1)} %get-tuple-element.58), channel_id=1, source_target_pairs={{2,0},{3,1},{4,2},{5,3},{6,4},{7,5},{0,6},{1,7},{10,8},{11,9},{12,... | collective-permute-start | bytes 786440 | tf_op jit(solution)/shard_map/ppermute | solution.py:246
  102.3 15.3 %collective-permute-start.10 = (bf16[4,128,256]{2,1,0:T(8,128)(2,1)}, bf16[4,128,256]{2,1,0:T(8,128)(2,1)S(1)}, u32[]{:S(2)}, u32[]{:S(2)}) collective-permute-start(bf16[4,128,256]{2,1,0:T(8,128)(2,1)} %get-tuple-element.59), channel_id=1, source_target_pairs={{6,0},{7,1},{0,2},{1,3},{2,4},{3,5},{4,6},{5,7},{14,8},{15,9},{8,1... | collective-permute-start | bytes 786440 | tf_op jit(solution)/shard_map/ppermute | solution.py:246
  104.2 14.2 %collective-permute-start.11 = (bf16[4,128,256]{2,1,0:T(8,128)(2,1)S(1)}, bf16[4,128,256]{2,1,0:T(8,128)(2,1)S(1)}, u32[]{:S(2)}, u32[]{:S(2)}) collective-permute-start(bf16[4,128,256]{2,1,0:T(8,128)(2,1)S(1)} %get-tuple-element.60), channel_id=1, source_target_pairs={{3,0},{2,1},{5,2},{4,3},{7,4},{6,5},{1,6},{0,7},{11,8},{10,9},{13,... | collective-permute-start | bytes 786440 | tf_op jit(solution)/shard_map/ppermute | solution.py:246
  108.7 21.4 %collective-permute-start.12 = (bf16[4,128,256]{2,1,0:T(8,128)(2,1)S(1)}, bf16[4,128,256]{2,1,0:T(8,128)(2,1)S(1)}, u32[]{:S(2)}, u32[]{:S(2)}) collective-permute-start(bf16[4,128,256]{2,1,0:T(8,128)(2,1)S(1)} %get-tuple-element.61), channel_id=1, source_target_pairs={{7,0},{6,1},{1,2},{0,3},{3,4},{2,5},{5,6},{4,7},{15,8},{14,9},{9,1... | collective-permute-start | bytes 786440 | tf_op jit(solution)/shard_map/ppermute | solution.py:246
  110.7 19.4 %collective-permute-start.13 = (bf16[4,128,256]{2,1,0:T(8,128)(2,1)S(1)}, bf16[4,128,256]{2,1,0:T(8,128)(2,1)S(1)}, u32[]{:S(2)}, u32[]{:S(2)}) collective-permute-start(bf16[4,128,256]{2,1,0:T(8,128)(2,1)S(1)} %get-tuple-element.62), channel_id=1, source_target_pairs={{1,0},{0,1},{3,2},{2,3},{5,4},{4,5},{7,6},{6,7},{9,8},{8,9},{11,10... | collective-permute-start | bytes 786440 | tf_op jit(solution)/shard_map/ppermute | solution.py:246
